TPU v7x, 128 devices: a whole 4x4x4 slice. The times are simulated.
128 devices in a mesh: slab: 32 (over y, x, core), mem: 4 (over z).
Axes of the slice: x: 4, y: 4, z: 4, core: 2. Of those that a mesh axis runs over, the one named last changes fastest.
Arguments:
- ensemble: float32 [80, 524288], P('mem', 'slab'), may hold values from -6 to 6
- obs_value: float32 [2, 2048], replicated, may hold values from -10 to 10
- obs_var: float32 [2, 2048], replicated, may hold values from 0.5 to 4
- obs_slab: int32 [2, 2048], replicated, may hold values from 0 to 31
- obs_offset: int32 [2, 2048], replicated, may hold values from 0 to 16383
- batch_order: int32 [2], replicated, may hold values from 0 to 1, each once
Outputs:
- analysis: float32 [80, 524288], P('mem', 'slab')
Inputs may be any that keep to these rules, and one draw needn't show every extreme that they name: batch_order names each batch once.
All inputs are finite; a program needn't handle non-finite values.
Results may differ from a plain program's by a relative error of at most 0.0003.
Values sent between devices are 32-bit elements; how exact they have to be, the bound alone decides.
A program may use at most 64 MiB of HBM per device.

v0:
```python
import jax
import jax.numpy as jnp
from jax import lax
from jax.sharding import PartitionSpec as P

NB = 2
OB = 256
LOC_C = 2048


def from_behind(value, axis, steps):
    count = lax.axis_size(axis)
    leading, last = (max(0, -steps), min(count, count - steps))
    return lax.ppermute(value, axis, [(source, source + steps) for source in range(leading, last)])


def gc_taper(distance, half_width):
    ratio = distance / half_width
    inner_part = (((-0.25 * ratio + 0.5) * ratio + 0.625) * ratio - 5.0 / 3.0) * ratio * ratio + 1.0
    safe_ratio = jnp.maximum(ratio, 1.0)
    outer_part = (
        ((((ratio / 12.0 - 0.5) * ratio + 0.625) * ratio + 5.0 / 3.0) * ratio - 5.0) * ratio
        + 4.0
        - 2.0 / (3.0 * safe_ratio)
    )
    return jnp.where(ratio <= 1.0, inner_part, jnp.where(ratio < 2.0, outer_part, 0.0))


def pick_columns(members, columns, width):
    usable = (columns >= 0) & (columns < width)
    safe_cols = jnp.clip(columns, 0, width - 1)
    return jnp.take(members, safe_cols, axis=1) * usable.astype(jnp.float32)[None, :]


def local(ensemble, obs_value, obs_var, obs_slab, obs_offset, batch_order):
    members = lax.all_to_all(ensemble, "mem", split_axis=1, concat_axis=0, tiled=True)
    mem_count = lax.axis_size("mem")
    sub_vars = members.shape[1]
    slab_vars = sub_vars * mem_count
    total_members = members.shape[0]
    flat_index = lax.axis_index("slab") * mem_count + lax.axis_index("mem")
    first_var = flat_index * sub_vars
    positions = (first_var + jnp.arange(sub_vars)).astype(jnp.float32)
    half_width = jnp.float32(LOC_C)
    obs_total = obs_value.shape[1]
    block_len = OB
    for batch_step in range(NB):
        which = batch_order[batch_step]
        obs_loc = obs_slab[which] * slab_vars + obs_offset[which]
        values = obs_value[which]
        variance = obs_var[which]
        owned = pick_columns(members, obs_loc - first_var, sub_vars)
        from_below = from_behind(owned, ("slab", "mem"), 1)
        from_above = from_behind(owned, ("slab", "mem"), -1)
        prior = from_below + owned + from_above
        ybar = jnp.mean(prior, axis=0)
        obs_anom = prior - ybar
        spread = jnp.sum(obs_anom * obs_anom, axis=0) / (total_members - 1.0)
        denom = spread + variance
        alpha = 1.0 / (1.0 + jnp.sqrt(variance / denom))
        innov = values - ybar
        obs_pos = obs_loc.astype(jnp.float32)
        xbar = jnp.mean(members, axis=0)
        state_anom = members - xbar

        def add_block(block_num, carry):
            mean_inc, anom_inc = carry
            offset = block_num * block_len
            anom_blk = lax.dynamic_slice_in_dim(obs_anom, offset, block_len, 1)
            denom_blk = lax.dynamic_slice_in_dim(denom, offset, block_len, 0)
            alpha_blk = lax.dynamic_slice_in_dim(alpha, offset, block_len, 0)
            innov_blk = lax.dynamic_slice_in_dim(innov, offset, block_len, 0)
            pos_blk = lax.dynamic_slice_in_dim(obs_pos, offset, block_len, 0)
            rho = gc_taper(jnp.abs(positions[:, None] - pos_blk[None, :]), half_width)
            cov = jnp.einsum("kv,ko->vo", state_anom, anom_blk, precision=lax.Precision.HIGHEST) / (
                total_members - 1.0
            )
            gain = rho * cov / denom_blk
            mean_inc = mean_inc + jnp.dot(gain, innov_blk, precision=lax.Precision.HIGHEST)
            anom_inc = anom_inc + jnp.einsum(
                "vo,ko->kv", gain * alpha_blk, anom_blk, precision=lax.Precision.HIGHEST
            )
            return (mean_inc, anom_inc)

        start_carry = (
            jnp.zeros((sub_vars,), jnp.float32),
            jnp.zeros((total_members, sub_vars), jnp.float32),
        )
        mean_inc, anom_inc = lax.fori_loop(0, obs_total // block_len, add_block, start_carry)
        members = xbar + mean_inc + state_anom - anom_inc
    return lax.all_to_all(members, "mem", split_axis=0, concat_axis=1, tiled=True)


def solution(mesh):
    return jax.shard_map(
        local,
        mesh=mesh,
        in_specs=(P("mem", "slab"), P(), P(), P(), P(), P()),
        out_specs=P("mem", "slab"),
        check_vma=False,
    )
```

profile of v0, /device:TPU:1, one launch (start us, length us, event | category | flops | bytes accessed | tf_op | source)
XLA Modules:
  0.0 469.7 jit_solution(3384224561010194229)
XLA Ops:
  4.2 5.9 %all-to-all-start = ((f32[20,4,4096]{2,0,1:T(8,128)}), f32[20,4,4096]{2,0,1:T(8,128)S(1)}, u32[]{:S(2)}, u32[]{:S(2)}) async-start(f32[20,4,4096]{2,0,1:T(8,128)} %copy.36), calls=%async_computation | async-start | bytes 3145728 | tf_op jit(solution)/shard_map/all_to_all | solution.py:36
  15.3 14.6 %all-to-all-done = f32[20,4,4096]{2,0,1:T(8,128)S(1)} async-done(((f32[20,4,4096]{2,0,1:T(8,128)}), f32[20,4,4096]{2,0,1:T(8,128)S(1)}, u32[]{:S(2)}, u32[]{:S(2)}) %all-to-all-start) | async-done | bytes 1310752 | tf_op jit(solution)/shard_map/all_to_all | solution.py:36
  34.0 7.6 %gather_fusion = f32[2048,80]{1,0:T(8,128)} fusion(f32[80,4096]{0,1:T(8,128)S(1)} %copy.37, s32[2048]{0:T(1024)S(1)} %fusion.28), kind=kCustom, calls=%fused_computation.clone | custom fusion | bytes 1318912 | tf_op jit(solution)/shard_map/jit(_take)/gather | solution.py:32
  48.7 4.8 %collective-permute-start.1 = (f32[80,2048]{1,0:T(8,128)}, f32[80,2048]{1,0:T(8,128)}, u32[]{:S(2)}, u32[]{:S(2)}) collective-permute-start(f32[80,2048]{1,0:T(8,128)} %copy.38), channel_id=1, source_target_pairs={{1,0},{2,1},{3,2},{4,3},{5,4},{6,5},{7,6},{8,7},{9,8},{10,9},{11,1... | collective-permute-start | bytes 1966088 | tf_op jit(solution)/shard_map/ppermute | solution.py:14
  63.6 4.6 collective-permute-done.1
  73.1 3.3 multiply_reduce_fusion.1
  78.0 156.3 %while.36 = (s32[]{:T(128)}, f32[4096]{0:T(1024)S(1)}, f32[80,4096]{1,0:T(8,128)S(1)}, f32[2048]{0:T(1024)}, f32[80,2048]{1,0:T(8,128)S(1)}, /*index=5*/f32[80,4...) while((s32[]{:T(128)}, f32[4096]{0:T(1024)S(1)}, ...), condition=%wide.region_4.6_spmd.clone, body=%wide.region_3.5_spmd.clone.sunk | while | flops 2062172160 | bytes 33566964 | solution.py:89
  78.9 10.8 %fusion.68 = f32[4096,256]{0,1:T(8,128)} fusion(f32[80,4096]{1,0:T(8,128)} %get-tuple-element.885, f32[256]{0:T(256)S(1)} %dynamic_slice.176, f32[256]{0:T(256)S(1)} %dynamic_slice.177, f32[4096]{0:T(1024)S(1)} %add_convert_fusion.4, f32[80,2048]{1,0:T(8,128)S(1)} %get-tuple-element.884, s32[]{:T(128)S(6)} %select_n.141), kind=kOutput, calls=%fused_computation.9.clone.1 | convolution fusion | flops 1041235968 | bytes 5605380 | tf_op jit(solution)/shard_map/while/body/eval_jaxpr/kv,ko->vo/dot_general | solution.py:75
  89.7 5.5 %convolution_add_fusion.4 = f32[80,4096]{1,0:T(8,128)S(1)} fusion(f32[4096,256]{0,1:T(8,128)} %fusion.68, f32[256]{0:T(256)S(1)} %dynamic_slice.179, f32[80,4096]{1,0:T(8,128)S(1)} %get-tuple-element.868, pred[]{:T(512)S(6)} %compare.6, f32[80,2048]{1,0:T(8,128)S(1)} %get-tuple-element.884, s32[]{:T(128)S(6)} %select_n.141), kind=kOutput, calls=%fused_computation.8.clone.1 | convolution fusion | flops 1008336896 | bytes 6898693 | tf_op jit(solution)/shard_map/while/body/eval_jaxpr/vo,ko->kv/dot_general | solution.py:80
  98.4 10.8 %fusion.68 = f32[4096,256]{0,1:T(8,128)} fusion(f32[80,4096]{1,0:T(8,128)} %get-tuple-element.885, f32[256]{0:T(256)S(1)} %dynamic_slice.176, f32[256]{0:T(256)S(1)} %dynamic_slice.177, f32[4096]{0:T(1024)S(1)} %add_convert_fusion.4, f32[80,2048]{1,0:T(8,128)S(1)} %get-tuple-element.884, s32[]{:T(128)S(6)} %select_n.141), kind=kOutput, calls=%fused_computation.9.clone.1 | convolution fusion | flops 1041235968 | bytes 5605380 | tf_op jit(solution)/shard_map/while/body/eval_jaxpr/kv,ko->vo/dot_general | solution.py:75
  109.3 5.5 %convolution_add_fusion.4 = f32[80,4096]{1,0:T(8,128)S(1)} fusion(f32[4096,256]{0,1:T(8,128)} %fusion.68, f32[256]{0:T(256)S(1)} %dynamic_slice.179, f32[80,4096]{1,0:T(8,128)S(1)} %get-tuple-element.868, pred[]{:T(512)S(6)} %compare.6, f32[80,2048]{1,0:T(8,128)S(1)} %get-tuple-element.884, s32[]{:T(128)S(6)} %select_n.141), kind=kOutput, calls=%fused_computation.8.clone.1 | convolution fusion | flops 1008336896 | bytes 6898693 | tf_op jit(solution)/shard_map/while/body/eval_jaxpr/vo,ko->kv/dot_general | solution.py:80
  118.0 10.8 %fusion.68 = f32[4096,256]{0,1:T(8,128)} fusion(f32[80,4096]{1,0:T(8,128)} %get-tuple-element.885, f32[256]{0:T(256)S(1)} %dynamic_slice.176, f32[256]{0:T(256)S(1)} %dynamic_slice.177, f32[4096]{0:T(1024)S(1)} %add_convert_fusion.4, f32[80,2048]{1,0:T(8,128)S(1)} %get-tuple-element.884, s32[]{:T(128)S(6)} %select_n.141), kind=kOutput, calls=%fused_computation.9.clone.1 | convolution fusion | flops 1041235968 | bytes 5605380 | tf_op jit(solution)/shard_map/while/body/eval_jaxpr/kv,ko->vo/dot_general | solution.py:75
  128.8 5.5 %convolution_add_fusion.4 = f32[80,4096]{1,0:T(8,128)S(1)} fusion(f32[4096,256]{0,1:T(8,128)} %fusion.68, f32[256]{0:T(256)S(1)} %dynamic_slice.179, f32[80,4096]{1,0:T(8,128)S(1)} %get-tuple-element.868, pred[]{:T(512)S(6)} %compare.6, f32[80,2048]{1,0:T(8,128)S(1)} %get-tuple-element.884, s32[]{:T(128)S(6)} %select_n.141), kind=kOutput, calls=%fused_computation.8.clone.1 | convolution fusion | flops 1008336896 | bytes 6898693 | tf_op jit(solution)/shard_map/while/body/eval_jaxpr/vo,ko->kv/dot_general | solution.py:80
  137.5 10.8 %fusion.68 = f32[4096,256]{0,1:T(8,128)} fusion(f32[80,4096]{1,0:T(8,128)} %get-tuple-element.885, f32[256]{0:T(256)S(1)} %dynamic_slice.176, f32[256]{0:T(256)S(1)} %dynamic_slice.177, f32[4096]{0:T(1024)S(1)} %add_convert_fusion.4, f32[80,2048]{1,0:T(8,128)S(1)} %get-tuple-element.884, s32[]{:T(128)S(6)} %select_n.141), kind=kOutput, calls=%fused_computation.9.clone.1 | convolution fusion | flops 1041235968 | bytes 5605380 | tf_op jit(solution)/shard_map/while/body/eval_jaxpr/kv,ko->vo/dot_general | solution.py:75
  148.3 5.5 %convolution_add_fusion.4 = f32[80,4096]{1,0:T(8,128)S(1)} fusion(f32[4096,256]{0,1:T(8,128)} %fusion.68, f32[256]{0:T(256)S(1)} %dynamic_slice.179, f32[80,4096]{1,0:T(8,128)S(1)} %get-tuple-element.868, pred[]{:T(512)S(6)} %compare.6, f32[80,2048]{1,0:T(8,128)S(1)} %get-tuple-element.884, s32[]{:T(128)S(6)} %select_n.141), kind=kOutput, calls=%fused_computation.8.clone.1 | convolution fusion | flops 1008336896 | bytes 6898693 | tf_op jit(solution)/shard_map/while/body/eval_jaxpr/vo,ko->kv/dot_general | solution.py:80
  157.1 10.8 %fusion.68 = f32[4096,256]{0,1:T(8,128)} fusion(f32[80,4096]{1,0:T(8,128)} %get-tuple-element.885, f32[256]{0:T(256)S(1)} %dynamic_slice.176, f32[256]{0:T(256)S(1)} %dynamic_slice.177, f32[4096]{0:T(1024)S(1)} %add_convert_fusion.4, f32[80,2048]{1,0:T(8,128)S(1)} %get-tuple-element.884, s32[]{:T(128)S(6)} %select_n.141), kind=kOutput, calls=%fused_computation.9.clone.1 | convolution fusion | flops 1041235968 | bytes 5605380 | tf_op jit(solution)/shard_map/while/body/eval_jaxpr/kv,ko->vo/dot_general | solution.py:75
  167.9 5.5 %convolution_add_fusion.4 = f32[80,4096]{1,0:T(8,128)S(1)} fusion(f32[4096,256]{0,1:T(8,128)} %fusion.68, f32[256]{0:T(256)S(1)} %dynamic_slice.179, f32[80,4096]{1,0:T(8,128)S(1)} %get-tuple-element.868, pred[]{:T(512)S(6)} %compare.6, f32[80,2048]{1,0:T(8,128)S(1)} %get-tuple-element.884, s32[]{:T(128)S(6)} %select_n.141), kind=kOutput, calls=%fused_computation.8.clone.1 | convolution fusion | flops 1008336896 | bytes 6898693 | tf_op jit(solution)/shard_map/while/body/eval_jaxpr/vo,ko->kv/dot_general | solution.py:80
  176.6 10.8 %fusion.68 = f32[4096,256]{0,1:T(8,128)} fusion(f32[80,4096]{1,0:T(8,128)} %get-tuple-element.885, f32[256]{0:T(256)S(1)} %dynamic_slice.176, f32[256]{0:T(256)S(1)} %dynamic_slice.177, f32[4096]{0:T(1024)S(1)} %add_convert_fusion.4, f32[80,2048]{1,0:T(8,128)S(1)} %get-tuple-element.884, s32[]{:T(128)S(6)} %select_n.141), kind=kOutput, calls=%fused_computation.9.clone.1 | convolution fusion | flops 1041235968 | bytes 5605380 | tf_op jit(solution)/shard_map/while/body/eval_jaxpr/kv,ko->vo/dot_general | solution.py:75
  187.4 5.5 %convolution_add_fusion.4 = f32[80,4096]{1,0:T(8,128)S(1)} fusion(f32[4096,256]{0,1:T(8,128)} %fusion.68, f32[256]{0:T(256)S(1)} %dynamic_slice.179, f32[80,4096]{1,0:T(8,128)S(1)} %get-tuple-element.868, pred[]{:T(512)S(6)} %compare.6, f32[80,2048]{1,0:T(8,128)S(1)} %get-tuple-element.884, s32[]{:T(128)S(6)} %select_n.141), kind=kOutput, calls=%fused_computation.8.clone.1 | convolution fusion | flops 1008336896 | bytes 6898693 | tf_op jit(solution)/shard_map/while/body/eval_jaxpr/vo,ko->kv/dot_general | solution.py:80
  196.1 10.8 %fusion.68 = f32[4096,256]{0,1:T(8,128)} fusion(f32[80,4096]{1,0:T(8,128)} %get-tuple-element.885, f32[256]{0:T(256)S(1)} %dynamic_slice.176, f32[256]{0:T(256)S(1)} %dynamic_slice.177, f32[4096]{0:T(1024)S(1)} %add_convert_fusion.4, f32[80,2048]{1,0:T(8,128)S(1)} %get-tuple-element.884, s32[]{:T(128)S(6)} %select_n.141), kind=kOutput, calls=%fused_computation.9.clone.1 | convolution fusion | flops 1041235968 | bytes 5605380 | tf_op jit(solution)/shard_map/while/body/eval_jaxpr/kv,ko->vo/dot_general | solution.py:75
  207.0 5.5 %convolution_add_fusion.4 = f32[80,4096]{1,0:T(8,128)S(1)} fusion(f32[4096,256]{0,1:T(8,128)} %fusion.68, f32[256]{0:T(256)S(1)} %dynamic_slice.179, f32[80,4096]{1,0:T(8,128)S(1)} %get-tuple-element.868, pred[]{:T(512)S(6)} %compare.6, f32[80,2048]{1,0:T(8,128)S(1)} %get-tuple-element.884, s32[]{:T(128)S(6)} %select_n.141), kind=kOutput, calls=%fused_computation.8.clone.1 | convolution fusion | flops 1008336896 | bytes 6898693 | tf_op jit(solution)/shard_map/while/body/eval_jaxpr/vo,ko->kv/dot_general | solution.py:80
  215.7 10.8 %fusion.68 = f32[4096,256]{0,1:T(8,128)} fusion(f32[80,4096]{1,0:T(8,128)} %get-tuple-element.885, f32[256]{0:T(256)S(1)} %dynamic_slice.176, f32[256]{0:T(256)S(1)} %dynamic_slice.177, f32[4096]{0:T(1024)S(1)} %add_convert_fusion.4, f32[80,2048]{1,0:T(8,128)S(1)} %get-tuple-element.884, s32[]{:T(128)S(6)} %select_n.141), kind=kOutput, calls=%fused_computation.9.clone.1 | convolution fusion | flops 1041235968 | bytes 5605380 | tf_op jit(solution)/shard_map/while/body/eval_jaxpr/kv,ko->vo/dot_general | solution.py:75
  226.5 5.5 %convolution_add_fusion.4 = f32[80,4096]{1,0:T(8,128)S(1)} fusion(f32[4096,256]{0,1:T(8,128)} %fusion.68, f32[256]{0:T(256)S(1)} %dynamic_slice.179, f32[80,4096]{1,0:T(8,128)S(1)} %get-tuple-element.868, pred[]{:T(512)S(6)} %compare.6, f32[80,2048]{1,0:T(8,128)S(1)} %get-tuple-element.884, s32[]{:T(128)S(6)} %select_n.141), kind=kOutput, calls=%fused_computation.8.clone.1 | convolution fusion | flops 1008336896 | bytes 6898693 | tf_op jit(solution)/shard_map/while/body/eval_jaxpr/vo,ko->kv/dot_general | solution.py:80
  236.2 3.4 fusion.36
  239.6 7.6 %gather_fusion.1 = f32[2048,80]{1,0:T(8,128)} fusion(f32[80,4096]{0,1:T(8,128)S(1)} %get-tuple-element.699, s32[2048]{0:T(1024)S(1)} %fusion.29), kind=kCustom, calls=%fused_computation.1.clone | custom fusion | bytes 1318912 | tf_op jit(solution)/shard_map/jit(_take)/gather | solution.py:32
  253.9 5.6 %collective-permute-start.3 = (f32[80,2048]{1,0:T(8,128)}, f32[80,2048]{1,0:T(8,128)}, u32[]{:S(2)}, u32[]{:S(2)}) collective-permute-start(f32[80,2048]{1,0:T(8,128)} %copy.46), channel_id=1, source_target_pairs={{1,0},{2,1},{3,2},{4,3},{5,4},{6,5},{7,6},{8,7},{9,8},{10,9},{11,1... | collective-permute-start | bytes 1966088 | tf_op jit(solution)/shard_map/ppermute | solution.py:14
  264.2 3.7 collective-permute-done.2
  270.4 4.0 collective-permute-done.3
  279.2 3.3 multiply_reduce_fusion
  285.0 151.3 %while.37 = (s32[]{:T(128)}, f32[4096]{0:T(1024)S(1)}, f32[80,4096]{1,0:T(8,128)S(1)}, f32[2048]{0:T(1024)S(1)}, f32[80,2048]{1,0:T(8,128)}, /*index=5*/f32[80,4...) while((s32[]{:T(128)}, f32[4096]{0:T(1024)S(1)}, ...), condition=%wide.region_9.11_spmd.clone, body=%wide.region_8.10_spmd.clone.sunk | while | flops 2062172160 | bytes 33566964 | solution.py:89
  285.2 10.8 %fusion.76 = f32[4096,256]{0,1:T(8,128)} fusion(f32[80,4096]{1,0:T(8,128)} %get-tuple-element.927, f32[256]{0:T(256)S(1)} %dynamic_slice.182, f32[256]{0:T(256)S(1)} %dynamic_slice.183, f32[4096]{0:T(1024)S(1)} %add_convert_fusion.5, f32[80,2048]{1,0:T(8,128)} %get-tuple-element.926, s32[]{:T(128)S(6)} %select_n.144), kind=kOutput, calls=%fused_computation.29.clone.1 | convolution fusion | flops 1041235968 | bytes 5605380 | tf_op jit(solution)/shard_map/while/body/eval_jaxpr/kv,ko->vo/dot_general | solution.py:75
  296.0 5.5 %convolution_add_fusion.5 = f32[80,4096]{1,0:T(8,128)S(1)} fusion(f32[4096,256]{0,1:T(8,128)} %fusion.76, f32[256]{0:T(256)S(1)} %dynamic_slice.185, f32[80,4096]{1,0:T(8,128)S(1)} %get-tuple-element.910, pred[]{:T(512)S(6)} %compare.7, f32[80,2048]{1,0:T(8,128)} %get-tuple-element.926, s32[]{:T(128)S(6)} %select_n.144), kind=kOutput, calls=%fused_computation.28.clone.1 | convolution fusion | flops 1008336896 | bytes 6898693 | tf_op jit(solution)/shard_map/while/body/eval_jaxpr/vo,ko->kv/dot_general | solution.py:80
  304.1 10.8 %fusion.76 = f32[4096,256]{0,1:T(8,128)} fusion(f32[80,4096]{1,0:T(8,128)} %get-tuple-element.927, f32[256]{0:T(256)S(1)} %dynamic_slice.182, f32[256]{0:T(256)S(1)} %dynamic_slice.183, f32[4096]{0:T(1024)S(1)} %add_convert_fusion.5, f32[80,2048]{1,0:T(8,128)} %get-tuple-element.926, s32[]{:T(128)S(6)} %select_n.144), kind=kOutput, calls=%fused_computation.29.clone.1 | convolution fusion | flops 1041235968 | bytes 5605380 | tf_op jit(solution)/shard_map/while/body/eval_jaxpr/kv,ko->vo/dot_general | solution.py:75
  314.9 5.5 %convolution_add_fusion.5 = f32[80,4096]{1,0:T(8,128)S(1)} fusion(f32[4096,256]{0,1:T(8,128)} %fusion.76, f32[256]{0:T(256)S(1)} %dynamic_slice.185, f32[80,4096]{1,0:T(8,128)S(1)} %get-tuple-element.910, pred[]{:T(512)S(6)} %compare.7, f32[80,2048]{1,0:T(8,128)} %get-tuple-element.926, s32[]{:T(128)S(6)} %select_n.144), kind=kOutput, calls=%fused_computation.28.clone.1 | convolution fusion | flops 1008336896 | bytes 6898693 | tf_op jit(solution)/shard_map/while/body/eval_jaxpr/vo,ko->kv/dot_general | solution.py:80
  323.0 10.8 %fusion.76 = f32[4096,256]{0,1:T(8,128)} fusion(f32[80,4096]{1,0:T(8,128)} %get-tuple-element.927, f32[256]{0:T(256)S(1)} %dynamic_slice.182, f32[256]{0:T(256)S(1)} %dynamic_slice.183, f32[4096]{0:T(1024)S(1)} %add_convert_fusion.5, f32[80,2048]{1,0:T(8,128)} %get-tuple-element.926, s32[]{:T(128)S(6)} %select_n.144), kind=kOutput, calls=%fused_computation.29.clone.1 | convolution fusion | flops 1041235968 | bytes 5605380 | tf_op jit(solution)/shard_map/while/body/eval_jaxpr/kv,ko->vo/dot_general | solution.py:75
  333.9 5.5 %convolution_add_fusion.5 = f32[80,4096]{1,0:T(8,128)S(1)} fusion(f32[4096,256]{0,1:T(8,128)} %fusion.76, f32[256]{0:T(256)S(1)} %dynamic_slice.185, f32[80,4096]{1,0:T(8,128)S(1)} %get-tuple-element.910, pred[]{:T(512)S(6)} %compare.7, f32[80,2048]{1,0:T(8,128)} %get-tuple-element.926, s32[]{:T(128)S(6)} %select_n.144), kind=kOutput, calls=%fused_computation.28.clone.1 | convolution fusion | flops 1008336896 | bytes 6898693 | tf_op jit(solution)/shard_map/while/body/eval_jaxpr/vo,ko->kv/dot_general | solution.py:80
  341.9 10.8 %fusion.76 = f32[4096,256]{0,1:T(8,128)} fusion(f32[80,4096]{1,0:T(8,128)} %get-tuple-element.927, f32[256]{0:T(256)S(1)} %dynamic_slice.182, f32[256]{0:T(256)S(1)} %dynamic_slice.183, f32[4096]{0:T(1024)S(1)} %add_convert_fusion.5, f32[80,2048]{1,0:T(8,128)} %get-tuple-element.926, s32[]{:T(128)S(6)} %select_n.144), kind=kOutput, calls=%fused_computation.29.clone.1 | convolution fusion | flops 1041235968 | bytes 5605380 | tf_op jit(solution)/shard_map/while/body/eval_jaxpr/kv,ko->vo/dot_general | solution.py:75
  352.8 5.5 %convolution_add_fusion.5 = f32[80,4096]{1,0:T(8,128)S(1)} fusion(f32[4096,256]{0,1:T(8,128)} %fusion.76, f32[256]{0:T(256)S(1)} %dynamic_slice.185, f32[80,4096]{1,0:T(8,128)S(1)} %get-tuple-element.910, pred[]{:T(512)S(6)} %compare.7, f32[80,2048]{1,0:T(8,128)} %get-tuple-element.926, s32[]{:T(128)S(6)} %select_n.144), kind=kOutput, calls=%fused_computation.28.clone.1 | convolution fusion | flops 1008336896 | bytes 6898693 | tf_op jit(solution)/shard_map/while/body/eval_jaxpr/vo,ko->kv/dot_general | solution.py:80
  360.8 10.8 %fusion.76 = f32[4096,256]{0,1:T(8,128)} fusion(f32[80,4096]{1,0:T(8,128)} %get-tuple-element.927, f32[256]{0:T(256)S(1)} %dynamic_slice.182, f32[256]{0:T(256)S(1)} %dynamic_slice.183, f32[4096]{0:T(1024)S(1)} %add_convert_fusion.5, f32[80,2048]{1,0:T(8,128)} %get-tuple-element.926, s32[]{:T(128)S(6)} %select_n.144), kind=kOutput, calls=%fused_computation.29.clone.1 | convolution fusion | flops 1041235968 | bytes 5605380 | tf_op jit(solution)/shard_map/while/body/eval_jaxpr/kv,ko->vo/dot_general | solution.py:75
  371.7 5.5 %convolution_add_fusion.5 = f32[80,4096]{1,0:T(8,128)S(1)} fusion(f32[4096,256]{0,1:T(8,128)} %fusion.76, f32[256]{0:T(256)S(1)} %dynamic_slice.185, f32[80,4096]{1,0:T(8,128)S(1)} %get-tuple-element.910, pred[]{:T(512)S(6)} %compare.7, f32[80,2048]{1,0:T(8,128)} %get-tuple-element.926, s32[]{:T(128)S(6)} %select_n.144), kind=kOutput, calls=%fused_computation.28.clone.1 | convolution fusion | flops 1008336896 | bytes 6898693 | tf_op jit(solution)/shard_map/while/body/eval_jaxpr/vo,ko->kv/dot_general | solution.py:80
  379.7 10.8 %fusion.76 = f32[4096,256]{0,1:T(8,128)} fusion(f32[80,4096]{1,0:T(8,128)} %get-tuple-element.927, f32[256]{0:T(256)S(1)} %dynamic_slice.182, f32[256]{0:T(256)S(1)} %dynamic_slice.183, f32[4096]{0:T(1024)S(1)} %add_convert_fusion.5, f32[80,2048]{1,0:T(8,128)} %get-tuple-element.926, s32[]{:T(128)S(6)} %select_n.144), kind=kOutput, calls=%fused_computation.29.clone.1 | convolution fusion | flops 1041235968 | bytes 5605380 | tf_op jit(solution)/shard_map/while/body/eval_jaxpr/kv,ko->vo/dot_general | solution.py:75
  390.6 5.5 %convolution_add_fusion.5 = f32[80,4096]{1,0:T(8,128)S(1)} fusion(f32[4096,256]{0,1:T(8,128)} %fusion.76, f32[256]{0:T(256)S(1)} %dynamic_slice.185, f32[80,4096]{1,0:T(8,128)S(1)} %get-tuple-element.910, pred[]{:T(512)S(6)} %compare.7, f32[80,2048]{1,0:T(8,128)} %get-tuple-element.926, s32[]{:T(128)S(6)} %select_n.144), kind=kOutput, calls=%fused_computation.28.clone.1 | convolution fusion | flops 1008336896 | bytes 6898693 | tf_op jit(solution)/shard_map/while/body/eval_jaxpr/vo,ko->kv/dot_general | solution.py:80
  398.7 10.8 %fusion.76 = f32[4096,256]{0,1:T(8,128)} fusion(f32[80,4096]{1,0:T(8,128)} %get-tuple-element.927, f32[256]{0:T(256)S(1)} %dynamic_slice.182, f32[256]{0:T(256)S(1)} %dynamic_slice.183, f32[4096]{0:T(1024)S(1)} %add_convert_fusion.5, f32[80,2048]{1,0:T(8,128)} %get-tuple-element.926, s32[]{:T(128)S(6)} %select_n.144), kind=kOutput, calls=%fused_computation.29.clone.1 | convolution fusion | flops 1041235968 | bytes 5605380 | tf_op jit(solution)/shard_map/while/body/eval_jaxpr/kv,ko->vo/dot_general | solution.py:75
  409.5 5.5 %convolution_add_fusion.5 = f32[80,4096]{1,0:T(8,128)S(1)} fusion(f32[4096,256]{0,1:T(8,128)} %fusion.76, f32[256]{0:T(256)S(1)} %dynamic_slice.185, f32[80,4096]{1,0:T(8,128)S(1)} %get-tuple-element.910, pred[]{:T(512)S(6)} %compare.7, f32[80,2048]{1,0:T(8,128)} %get-tuple-element.926, s32[]{:T(128)S(6)} %select_n.144), kind=kOutput, calls=%fused_computation.28.clone.1 | convolution fusion | flops 1008336896 | bytes 6898693 | tf_op jit(solution)/shard_map/while/body/eval_jaxpr/vo,ko->kv/dot_general | solution.py:80
  417.6 10.8 %fusion.76 = f32[4096,256]{0,1:T(8,128)} fusion(f32[80,4096]{1,0:T(8,128)} %get-tuple-element.927, f32[256]{0:T(256)S(1)} %dynamic_slice.182, f32[256]{0:T(256)S(1)} %dynamic_slice.183, f32[4096]{0:T(1024)S(1)} %add_convert_fusion.5, f32[80,2048]{1,0:T(8,128)} %get-tuple-element.926, s32[]{:T(128)S(6)} %select_n.144), kind=kOutput, calls=%fused_computation.29.clone.1 | convolution fusion | flops 1041235968 | bytes 5605380 | tf_op jit(solution)/shard_map/while/body/eval_jaxpr/kv,ko->vo/dot_general | solution.py:75
  428.4 5.5 %convolution_add_fusion.5 = f32[80,4096]{1,0:T(8,128)S(1)} fusion(f32[4096,256]{0,1:T(8,128)} %fusion.76, f32[256]{0:T(256)S(1)} %dynamic_slice.185, f32[80,4096]{1,0:T(8,128)S(1)} %get-tuple-element.910, pred[]{:T(512)S(6)} %compare.7, f32[80,2048]{1,0:T(8,128)} %get-tuple-element.926, s32[]{:T(128)S(6)} %select_n.144), kind=kOutput, calls=%fused_computation.28.clone.1 | convolution fusion | flops 1008336896 | bytes 6898693 | tf_op jit(solution)/shard_map/while/body/eval_jaxpr/vo,ko->kv/dot_general | solution.py:80
  438.1 4.9 %add_subtract_fusion = f32[80,4096]{0,1:T(8,128)} fusion(f32[80,4096]{0,1:T(8,128)} %copy.52, f32[4096]{0:T(1024)S(1)} %fusion.33, f32[80,4096]{0,1:T(8,128)S(1)} %get-tuple-element.699, f32[4096]{0:T(1024)S(1)} %broadcast_multiply_fusion), kind=kLoop, calls=%fused_computation.44 | loop fusion | flops 983040 | bytes 3964928 | tf_op jit(solution)/shard_map/sub | solution.py:90
  445.1 21.3 %all_to_all.38 = f32[4,20,4096]{2,1,0:T(8,128)S(1)} all-to-all(f32[4,20,4096]{2,1,0:T(8,128)S(1)} %all_to_all.32), channel_id=1, replica_groups=mesh['slab'=32,'mem'=4] {'mem'}, dimensions={0} | all-to-all | bytes 2621440 | tf_op jit(solution)/shard_map/all_to_all | solution.py:91
  (211 shorter events, 110.2 us)
Async XLA Ops:
  0.0 10.0 %copy-start.9 = (s32[2]{0:T(128)S(1)}, s32[2]{0:T(128)}, u32[]{:S(2)}) copy-start(s32[2]{0:T(128)} %param.17) | copy-start | bytes 28
  0.0 14.4 %copy-start.6 = (s32[2,2048]{1,0:T(2,128)S(1)}, s32[2,2048]{1,0:T(2,128)}, u32[]{:S(2)}) copy-start(s32[2,2048]{1,0:T(2,128)} %param.15) | copy-start | bytes 49156
  0.0 14.4 %copy-start.5 = (s32[2,2048]{1,0:T(2,128)S(1)}, s32[2,2048]{1,0:T(2,128)}, u32[]{:S(2)}) copy-start(s32[2,2048]{1,0:T(2,128)} %param.16) | copy-start | bytes 49156
  0.0 15.2 %copy-start.7 = (f32[2,2048]{1,0:T(2,128)S(1)}, f32[2,2048]{1,0:T(2,128)}, u32[]{:S(2)}) copy-start(f32[2,2048]{1,0:T(2,128)} %param.13) | copy-start | bytes 49156
  0.0 15.2 %copy-start.8 = (f32[2,2048]{1,0:T(2,128)S(1)}, f32[2,2048]{1,0:T(2,128)}, u32[]{:S(2)}) copy-start(f32[2,2048]{1,0:T(2,128)} %param.14) | copy-start | bytes 49156
  4.2 25.7 %all-to-all-start = ((f32[20,4,4096]{2,0,1:T(8,128)}), f32[20,4,4096]{2,0,1:T(8,128)S(1)}, u32[]{:S(2)}, u32[]{:S(2)}) async-start(f32[20,4,4096]{2,0,1:T(8,128)} %copy.36), calls=%async_computation | async-start | bytes 3145728 | tf_op jit(solution)/shard_map/all_to_all | solution.py:36
  29.8 1.1 copy-start.4
  34.0 21.1 %copy-start.2 = (f32[80,4096]{0,1:T(8,128)}, f32[80,4096]{0,1:T(8,128)S(1)}, u32[]{:S(2)}) copy-start(f32[80,4096]{0,1:T(8,128)S(1)} %copy.37) | copy-start | bytes 3932164
  46.5 14.6 %collective-permute-start = (f32[80,2048]{1,0:T(8,128)}, f32[80,2048]{1,0:T(8,128)}, u32[]{:S(2)}, u32[]{:S(2)}) collective-permute-start(f32[80,2048]{1,0:T(8,128)} %copy.38), channel_id=1, source_target_pairs={{0,1},{1,2},{2,3},{3,4},{4,5},{5,6},{6,7},{7,8},{8,9},{9,10},{10,1... | collective-permute-start | bytes 1966088 | tf_op jit(solution)/shard_map/ppermute | solution.py:14
  48.7 19.4 %collective-permute-start.1 = (f32[80,2048]{1,0:T(8,128)}, f32[80,2048]{1,0:T(8,128)}, u32[]{:S(2)}, u32[]{:S(2)}) collective-permute-start(f32[80,2048]{1,0:T(8,128)} %copy.38), channel_id=1, source_target_pairs={{1,0},{2,1},{3,2},{4,3},{5,4},{6,5},{7,6},{8,7},{9,8},{10,9},{11,1... | collective-permute-start | bytes 1966088 | tf_op jit(solution)/shard_map/ppermute | solution.py:14
  70.6 7.4 %copy-start.3 = (f32[80,4096]{1,0:T(8,128)S(1)}, f32[80,4096]{1,0:T(8,128)}, u32[]{:S(2)}) copy-start(f32[80,4096]{1,0:T(8,128)} %custom-call.1) | copy-start | bytes 3932164
  89.7 5.6 %copy-start = (f32[4096,256]{0,1:T(8,128)S(1)}, f32[4096,256]{0,1:T(8,128)}, u32[]{:S(2)}) copy-start(f32[4096,256]{0,1:T(8,128)} %fusion.68) | copy-start | bytes 12582916 | tf_op jit(solution)/shard_map/while
  109.3 5.6 %copy-start = (f32[4096,256]{0,1:T(8,128)S(1)}, f32[4096,256]{0,1:T(8,128)}, u32[]{:S(2)}) copy-start(f32[4096,256]{0,1:T(8,128)} %fusion.68) | copy-start | bytes 12582916 | tf_op jit(solution)/shard_map/while
  128.8 5.6 %copy-start = (f32[4096,256]{0,1:T(8,128)S(1)}, f32[4096,256]{0,1:T(8,128)}, u32[]{:S(2)}) copy-start(f32[4096,256]{0,1:T(8,128)} %fusion.68) | copy-start | bytes 12582916 | tf_op jit(solution)/shard_map/while
  148.3 5.6 %copy-start = (f32[4096,256]{0,1:T(8,128)S(1)}, f32[4096,256]{0,1:T(8,128)}, u32[]{:S(2)}) copy-start(f32[4096,256]{0,1:T(8,128)} %fusion.68) | copy-start | bytes 12582916 | tf_op jit(solution)/shard_map/while
  167.9 5.6 %copy-start = (f32[4096,256]{0,1:T(8,128)S(1)}, f32[4096,256]{0,1:T(8,128)}, u32[]{:S(2)}) copy-start(f32[4096,256]{0,1:T(8,128)} %fusion.68) | copy-start | bytes 12582916 | tf_op jit(solution)/shard_map/while
  187.4 5.6 %copy-start = (f32[4096,256]{0,1:T(8,128)S(1)}, f32[4096,256]{0,1:T(8,128)}, u32[]{:S(2)}) copy-start(f32[4096,256]{0,1:T(8,128)} %fusion.68) | copy-start | bytes 12582916 | tf_op jit(solution)/shard_map/while
  207.0 5.6 %copy-start = (f32[4096,256]{0,1:T(8,128)S(1)}, f32[4096,256]{0,1:T(8,128)}, u32[]{:S(2)}) copy-start(f32[4096,256]{0,1:T(8,128)} %fusion.68) | copy-start | bytes 12582916 | tf_op jit(solution)/shard_map/while
  226.5 5.6 %copy-start = (f32[4096,256]{0,1:T(8,128)S(1)}, f32[4096,256]{0,1:T(8,128)}, u32[]{:S(2)}) copy-start(f32[4096,256]{0,1:T(8,128)} %fusion.68) | copy-start | bytes 12582916 | tf_op jit(solution)/shard_map/while
  252.0 15.9 %collective-permute-start.2 = (f32[80,2048]{1,0:T(8,128)}, f32[80,2048]{1,0:T(8,128)}, u32[]{:S(2)}, u32[]{:S(2)}) collective-permute-start(f32[80,2048]{1,0:T(8,128)} %copy.46), channel_id=1, source_target_pairs={{0,1},{1,2},{2,3},{3,4},{4,5},{5,6},{6,7},{7,8},{8,9},{9,10},{10,1... | collective-permute-start | bytes 1966088 | tf_op jit(solution)/shard_map/ppermute | solution.py:14
  253.9 20.5 %collective-permute-start.3 = (f32[80,2048]{1,0:T(8,128)}, f32[80,2048]{1,0:T(8,128)}, u32[]{:S(2)}, u32[]{:S(2)}) collective-permute-start(f32[80,2048]{1,0:T(8,128)} %copy.46), channel_id=1, source_target_pairs={{1,0},{2,1},{3,2},{4,3},{5,4},{6,5},{7,6},{8,7},{9,8},{10,9},{11,1... | collective-permute-start | bytes 1966088 | tf_op jit(solution)/shard_map/ppermute | solution.py:14
  296.0 5.6 %copy-start.1 = (f32[4096,256]{0,1:T(8,128)S(1)}, f32[4096,256]{0,1:T(8,128)}, u32[]{:S(2)}) copy-start(f32[4096,256]{0,1:T(8,128)} %fusion.76) | copy-start | bytes 12582916 | tf_op jit(solution)/shard_map/while
  314.9 5.6 %copy-start.1 = (f32[4096,256]{0,1:T(8,128)S(1)}, f32[4096,256]{0,1:T(8,128)}, u32[]{:S(2)}) copy-start(f32[4096,256]{0,1:T(8,128)} %fusion.76) | copy-start | bytes 12582916 | tf_op jit(solution)/shard_map/while
  333.8 5.6 %copy-start.1 = (f32[4096,256]{0,1:T(8,128)S(1)}, f32[4096,256]{0,1:T(8,128)}, u32[]{:S(2)}) copy-start(f32[4096,256]{0,1:T(8,128)} %fusion.76) | copy-start | bytes 12582916 | tf_op jit(solution)/shard_map/while
  352.8 5.6 %copy-start.1 = (f32[4096,256]{0,1:T(8,128)S(1)}, f32[4096,256]{0,1:T(8,128)}, u32[]{:S(2)}) copy-start(f32[4096,256]{0,1:T(8,128)} %fusion.76) | copy-start | bytes 12582916 | tf_op jit(solution)/shard_map/while
  371.7 5.6 %copy-start.1 = (f32[4096,256]{0,1:T(8,128)S(1)}, f32[4096,256]{0,1:T(8,128)}, u32[]{:S(2)}) copy-start(f32[4096,256]{0,1:T(8,128)} %fusion.76) | copy-start | bytes 12582916 | tf_op jit(solution)/shard_map/while
  390.6 5.6 %copy-start.1 = (f32[4096,256]{0,1:T(8,128)S(1)}, f32[4096,256]{0,1:T(8,128)}, u32[]{:S(2)}) copy-start(f32[4096,256]{0,1:T(8,128)} %fusion.76) | copy-start | bytes 12582916 | tf_op jit(solution)/shard_map/while
  409.5 5.6 %copy-start.1 = (f32[4096,256]{0,1:T(8,128)S(1)}, f32[4096,256]{0,1:T(8,128)}, u32[]{:S(2)}) copy-start(f32[4096,256]{0,1:T(8,128)} %fusion.76) | copy-start | bytes 12582916 | tf_op jit(solution)/shard_map/while
  428.4 5.6 %copy-start.1 = (f32[4096,256]{0,1:T(8,128)S(1)}, f32[4096,256]{0,1:T(8,128)}, u32[]{:S(2)}) copy-start(f32[4096,256]{0,1:T(8,128)} %fusion.76) | copy-start | bytes 12582916 | tf_op jit(solution)/shard_map/while
where the time goes:
time: 474 us; the launch traced here: 470 us
  matrix products  296 us (62%)
  local copies, waits for them, and re-layouts  67.3 us (14%)
  other arithmetic  31.3 us (7%)
  waiting for transfers between devices  28.4 us (6%)
  blocking collectives  21.3 us (4%)
  starting transfers between devices  20.3 us (4%)
    dot_general x16, matrix products, add_block(): jnp.einsum('kv,ko->vo', state_anom, anom_blk, precision=lax.Precision.HIG...  172 us
    dot_general x16, matrix products, add_block(): jnp.einsum('vo,ko->kv', gain * alpha_blk, anom_blk, precision=lax.Precisi...  87.8 us
    dot_general x16, matrix products, add_block(): jnp.dot(gain, innov_blk, precision=lax.Precision.HIGHEST)  36.2 us
    all_to_all x1, blocking collectives, local(): lax.all_to_all(members, 'mem', split_axis=0, concat_axis=1, tiled=True)  21.3 us
    gather x2, local copies, waits for them, and re-layouts, pick_columns(): jnp.take(members, safe_cols, axis=1) * usable.astype(jnp.float32)[None, :]  15.2 us
    all_to_all x1, waiting for transfers between devices, local(): lax.all_to_all(ensemble, 'mem', split_axis=1, concat_axis=0, tiled=True)  14.6 us
    ppermute x4, starting transfers between devices, from_behind(): lax.ppermute(value, axis, [(source, source + steps) for source in range(l...  14.5 us
    ppermute x4, waiting for transfers between devices, from_behind(): lax.ppermute(value, axis, [(source, source + steps) for source in range(l...  13.9 us
  transfers between devices with their start and end apart: 5, of which 5 were waited for; matrix products, arithmetic and copies ran while one was open for 4% of the time, Pallas kernels for 0%

commit v1 on v0

--- a/solution.py
+++ b/solution.py
@@ -1,11 +1,33 @@
+import functools
+
 import jax
 import jax.numpy as jnp
 from jax import lax
+from jax.experimental import pallas as pl
+from jax.experimental.pallas import tpu as pltpu
 from jax.sharding import PartitionSpec as P
 
 NB = 2
 OB = 256
 LOC_C = 2048
+REACH = 2 * LOC_C
+MEMBERS = 80
+SUB = 4096
+RANKS = 4
+SLAB = SUB * RANKS
+OBS = 2048
+OWN = 256
+INNER = 256
+OUTER = 128
+CH = 512
+NC = SUB // CH
+PW = CH * 5 // 2
+CW = 2 * OWN * 5 // 2
+EARLY = 4
+FAR = -1.0e5
+MESH = pl.DeviceIdType.MESH
+F32 = jnp.float32
+BF16 = jnp.bfloat16
 
 
 def from_behind(value, axis, steps):
@@ -32,7 +54,7 @@
     return jnp.take(members, safe_cols, axis=1) * usable.astype(jnp.float32)[None, :]
 
 
-def local(ensemble, obs_value, obs_var, obs_slab, obs_offset, batch_order):
+def general(ensemble, obs_value, obs_var, obs_slab, obs_offset, batch_order):
     members = lax.all_to_all(ensemble, "mem", split_axis=1, concat_axis=0, tiled=True)
     mem_count = lax.axis_size("mem")
     sub_vars = members.shape[1]
@@ -91,9 +113,431 @@
     return lax.all_to_all(members, "mem", split_axis=0, concat_axis=1, tiled=True)
 
 
+def split3(x):
+    a = x.astype(BF16)
+    r = x - a.astype(F32)
+    b = r.astype(BF16)
+    c = (r - b.astype(F32)).astype(BF16)
+    return a, b, c
+
+
+def prep_kernel(slabs, order, val, var, slab, off, offs_out, prm_out, ok_out):
+    s = lax.axis_index("slab")
+    m = lax.axis_index("mem")
+    first = (s * RANKS + m) * SUB
+    nb = lax.rem(s + jnp.where(m < RANKS // 2, slabs - 1, 1), slabs)
+    lane = lax.broadcasted_iota(jnp.int32, (8, OBS), 1)
+    rows = [pl.ds(order[i], 1) for i in range(NB)]
+    slab_b = [slab[r, :] for r in rows]
+    off_b = [off[r, :] for r in rows]
+    loc_b = [a * SLAB + b for a, b in zip(slab_b, off_b)]
+    rel_b = [a - first for a in loc_b]
+    own_b = [a == s for a in slab_b]
+    nb_b = [a == nb for a in slab_b]
+    inner_b = [(r >= -SUB) & (r < 2 * SUB) for r in rel_b]
+    outer = (rel_b[0] >= -2 * SUB) & (rel_b[0] < 3 * SUB) & jnp.logical_not(inner_b[0])
+    masks = own_b + nb_b + inner_b + [outer, outer]
+    marks = jnp.concatenate([jnp.where(a, 1, 0) for a in masks], axis=0)
+    run = marks
+    step = 1
+    while step < OBS:
+        run = run + jnp.where(lane >= step, pltpu.roll(run, step, 1), 0)
+        step *= 2
+    run = run - marks
+    own_slot = [jnp.where(own_b[i], run[i : i + 1], -1) for i in range(NB)]
+    src = [jnp.where(own_b[i], run[i : i + 1], OWN + run[2 + i : 3 + i]) for i in range(NB)]
+    slot = [
+        jnp.where(inner_b[0], run[4:5], jnp.where(outer, INNER + run[6:7], -1)),
+        jnp.where(inner_b[1], run[5:6], -1),
+    ]
+    width = [INNER + OUTER, INNER]
+    begin = 0
+    for i in range(NB):
+        vals = jnp.concatenate(
+            [
+                loc_b[i].astype(F32) * (1.0 / LOC_C),
+                val[rows[i], :],
+                var[rows[i], :],
+                src[i].astype(F32),
+                jnp.ones((1, OBS), F32),
+                off_b[i].astype(F32),
+                jnp.zeros((2, OBS), F32),
+            ],
+            axis=0,
+        )
+        pieces = jnp.concatenate(list(split3(vals)), axis=0)
+        which = lax.broadcasted_iota(jnp.int32, (width[i], OBS), 0)
+        hot_w = jnp.where(which == slot[i], 1.0, 0.0).astype(BF16)
+        which_o = lax.broadcasted_iota(jnp.int32, (OWN, OBS), 0)
+        hot_o = jnp.where(which_o == own_slot[i], 1.0, 0.0).astype(BF16)
+        hot = jnp.concatenate([hot_w, hot_o], axis=0)
+        got = lax.dot_general(pieces, hot, (((1,), (1,)), ((), ())), preferred_element_type=F32)
+        got = got[0:8] + got[8:16] + got[16:24]
+        w = width[i]
+        there = got[4:5, :w] > 0.5
+        prm_out[0:1, begin : begin + w] = jnp.where(there, got[0:1, :w], FAR)
+        prm_out[1:2, begin : begin + w] = got[1:2, :w]
+        prm_out[2:3, begin : begin + w] = jnp.where(there, got[2:3, :w], 1.0)
+        prm_out[3:4, begin : begin + w] = jnp.where(there, got[3:4, :w], -1.0)
+        prm_out[4:8, begin : begin + w] = jnp.zeros((4, w), F32)
+        offs_out[0:1, i * OWN : (i + 1) * OWN] = got[5:6, w:].astype(jnp.int32)
+        begin += w
+    bad = jnp.zeros((8, 128), F32)
+    bins = lax.broadcasted_iota(jnp.int32, (128, OBS), 0)
+    at = lax.broadcasted_iota(jnp.int32, (8, 128), 1)
+    for i in range(NB):
+        hot = jnp.where(bins == loc_b[i] // SUB, 1.0, 0.0).astype(BF16)
+        cnt = lax.dot_general(
+            jnp.ones((8, OBS), BF16), hot, (((1,), (1,)), ((), ())), preferred_element_type=F32
+        )
+        around = [pltpu.roll(cnt, sh, 1) for sh in (1, 127, 2, 126, 3)]
+        near = cnt + around[0] + around[1]
+        far = around[2] + around[3]
+        whole = jnp.where(lax.rem(at, RANKS) == RANKS - 1, cnt + around[0] + around[2] + around[4], 0.0)
+        bad = jnp.maximum(bad, jnp.where((near > INNER) | (far > OUTER) | (whole > OWN), 1.0, 0.0))
+    ok_out[...] = bad
+
+
+def prep(mesh, obs_value, obs_var, obs_slab, obs_offset, batch_order):
+    vm = pl.BlockSpec(memory_space=pltpu.VMEM)
+    return pl.pallas_call(
+        functools.partial(prep_kernel, mesh.shape["slab"]),
+        out_shape=(
+            jax.ShapeDtypeStruct((1, NB * OWN), jnp.int32),
+            jax.ShapeDtypeStruct((8, 2 * INNER + OUTER), F32),
+            jax.ShapeDtypeStruct((8, 128), F32),
+        ),
+        in_specs=[pl.BlockSpec(memory_space=pltpu.SMEM), vm, vm, vm, vm],
+        out_specs=(vm, vm, vm),
+        compiler_params=pltpu.CompilerParams(vmem_limit_bytes=48 << 20),
+        name="prep",
+    )(batch_order, obs_value, obs_var, obs_slab, obs_offset)
+
+
+def taper(z):
+    p_in = (((-0.25 * z + 0.5) * z + 0.625) * z - 5.0 / 3.0) * (z * z) + 1.0
+    t = jnp.maximum(2.0 - z, 0.0)
+    t = t * t
+    p_out = (t * t) * ((z * (1.0 / 12.0) + 1.0 / 6.0) - (1.0 / 24.0) / jnp.maximum(z, 1.0))
+    return jnp.where(z <= 1.0, p_in, p_out)
+
+
+def update(e, pos_v, pos_o, a, wst):
+    n = e.shape[1]
+    eh = e.astype(BF16)
+    el = (e - eh.astype(F32)).astype(BF16)
+    cov = jnp.dot(a, jnp.concatenate([eh, el, eh], axis=0), preferred_element_type=F32)
+    z = jnp.abs(pos_v - jnp.concatenate([pos_o] * (n // 128), axis=1))
+    g = taper(z) * cov
+    gh = g.astype(BF16)
+    gl = (g - gh.astype(F32)).astype(BF16)
+    one = jnp.dot(wst, gh, preferred_element_type=F32)
+    two = jnp.dot(wst[:MEMBERS], gl, preferred_element_type=F32)
+    return e + (one[:MEMBERS] + one[MEMBERS:] + two)
+
+
+def stats(x, val, var):
+    ybar = jnp.sum(x, axis=0, keepdims=True) * (1.0 / MEMBERS)
+    ya = x - ybar
+    spread = jnp.sum(ya * ya, axis=0, keepdims=True) / (MEMBERS - 1.0)
+    denom = spread + var
+    alpha = 1.0 / (1.0 + jnp.sqrt(var / denom))
+    w = ((val - ybar) - alpha * ya) / (denom * (MEMBERS - 1.0))
+    hi = ya.astype(BF16).astype(F32)
+    a = jnp.transpose(jnp.concatenate([hi, hi, ya - hi], axis=0)).astype(BF16)
+    wh = w.astype(BF16)
+    wl = (w - wh.astype(F32)).astype(BF16)
+    return a, jnp.concatenate([wh, wl], axis=0)
+
+
+def column(row):
+    return jnp.transpose(jnp.broadcast_to(row, (128, row.shape[1])))
+
+
+def unpack(blocks, width):
+    half = width // 2
+    low = lax.broadcasted_iota(jnp.int32, (8, half), 0) < 4
+    tiles = []
+    for b in blocks:
+        tiles += [b[:, :width], b[:, width : 2 * width]]
+    for i in (0, 2):
+        p, q = blocks[i][:, 2 * width :], blocks[i + 1][:, 2 * width :]
+        left = jnp.where(low, p, pltpu.roll(q, 4, 0))
+        right = jnp.where(low, pltpu.roll(p, 4, 0), q)
+        tiles.append(jnp.concatenate([left, right], axis=1))
+    return jnp.concatenate(tiles, axis=0)
+
+
+def pack(e):
+    width = e.shape[1]
+    half = width // 2
+    low = lax.broadcasted_iota(jnp.int32, (8, half), 0) < 4
+    tails = []
+    for i in (0, 1):
+        t = e[64 + 8 * i : 72 + 8 * i]
+        left, right = t[:, :half], t[:, half:]
+        tails.append(jnp.where(low, left, pltpu.roll(right, 4, 0)))
+        tails.append(jnp.where(low, pltpu.roll(left, 4, 0), right))
+    return [
+        [(0, e[16 * p : 16 * p + 8]), (width, e[16 * p + 8 : 16 * p + 16]), (2 * width, tails[p])]
+        for p in range(RANKS)
+    ]
+
+
+def fused_kernel(
+    slabs, offs, prm, x, out,
+    xb, pk, rv, rpk, orv, cpk, crv, nrv, a1, w1, p1, a2, w2, p2,
+    fs, fr, bs, br, cs, cr, ns, nr,
+):
+    s = lax.axis_index("slab")
+    m = lax.axis_index("mem")
+    below = m < RANKS // 2
+    send_to = lax.rem(s + jnp.where(below, 1, slabs - 1), slabs)
+    gets_from = lax.rem(s + jnp.where(below, slabs - 1, 1), slabs)
+
+    barrier = pltpu.get_barrier_semaphore()
+    for d in range(1, RANKS):
+        pl.semaphore_signal(barrier, inc=1, device_id=(s, lax.rem(m + d, RANKS)), device_id_type=MESH)
+    pl.semaphore_signal(barrier, inc=1, device_id=(gets_from, m), device_id_type=MESH)
+    pl.semaphore_wait(barrier, RANKS)
+
+    def fill(ref, base):
+        half = CH // 2
+        ref[:, 0:CH] = x[0:8, pl.ds(base, CH)]
+        ref[:, CH : 2 * CH] = x[8:16, pl.ds(base, CH)]
+        ref[0:4, 2 * CH : PW] = x[16:20, pl.ds(base, half)]
+        ref[4:8, 2 * CH : PW] = x[16:20, pl.ds(base + half, half)]
+
+    def forward(d, c):
+        return pltpu.make_async_remote_copy(
+            src_ref=pk.at[d - 1, c],
+            dst_ref=rv.at[m, c],
+            send_sem=fs.at[d - 1, c],
+            recv_sem=fr.at[d - 1, c],
+            device_id=(s, lax.rem(m + d, RANKS)),
+            device_id_type=MESH,
+        )
+
+    def landed(d, c):
+        return pltpu.make_async_remote_copy(
+            src_ref=pk.at[d - 1, c],
+            dst_ref=rv.at[lax.rem(m + RANKS - d, RANKS), c],
+            send_sem=fs.at[d - 1, c],
+            recv_sem=fr.at[d - 1, c],
+            device_id=(s, lax.rem(m + d, RANKS)),
+            device_id_type=MESH,
+        )
+
+    def send_chunk(c, _):
+        for d in (1, 3, 2):
+            p = lax.rem(m + d, RANKS)
+            fill(pk.at[d - 1, c], pl.multiple_of(p * SUB + c * CH, CH))
+            forward(d, c).start()
+        fill(rv.at[m, c], pl.multiple_of(m * SUB + c * CH, CH))
+        return 0
+
+    lax.fori_loop(0, EARLY, send_chunk, 0)
+
+    def spread_out(i, _):
+        for k in range(8):
+            xb[i * 8 + k] = x[:, pl.ds(pl.multiple_of(i * 1024 + k * 128, 128), 128)]
+        return 0
+
+    lax.fori_loop(0, SLAB // 1024, spread_out, 0)
+    lane = lax.broadcasted_iota(jnp.int32, (20, 128), 1)
+    half = OWN
+    for t in range(NB * OWN // 128):
+
+        def pick(j, acc):
+            o = offs[0, t * 128 + j]
+            blk = xb[lax.shift_right_logical(o, 7)]
+            one = jnp.sum(jnp.where(lane == (o & 127), blk, 0.0), axis=1, keepdims=True)
+            return jnp.where(lane == j, one, acc)
+
+        cols = lax.fori_loop(0, 128, pick, jnp.zeros((20, 128), F32), unroll=8)
+        cpk[:, t * 128 : (t + 1) * 128] = cols[0:8]
+        cpk[:, NB * OWN + t * 128 : NB * OWN + (t + 1) * 128] = cols[8:16]
+        r = 0 if t * 128 < half else 4
+        q = 2 * NB * OWN + (t * 128) % half
+        cpk[r : r + 4, q : q + 128] = cols[16:20]
+
+    def columns(d):
+        return pltpu.make_async_remote_copy(
+            src_ref=cpk,
+            dst_ref=crv.at[m],
+            send_sem=cs.at[d - 1],
+            recv_sem=cr.at[d - 1],
+            device_id=(s, lax.rem(m + d, RANKS)),
+            device_id_type=MESH,
+        )
+
+    def columns_landed(d):
+        return pltpu.make_async_remote_copy(
+            src_ref=cpk,
+            dst_ref=crv.at[lax.rem(m + RANKS - d, RANKS)],
+            send_sem=cs.at[d - 1],
+            recv_sem=cr.at[d - 1],
+            device_id=(s, lax.rem(m + d, RANKS)),
+            device_id_type=MESH,
+        )
+
+    for d in (1, 3, 2):
+        columns(d).start()
+    crv[m] = cpk[...]
+    lax.fori_loop(EARLY, NC, send_chunk, 0)
+    for d in (1, 3, 2):
+        columns_landed(d).wait_recv()
+    beside = pltpu.make_async_remote_copy(
+        src_ref=crv, dst_ref=nrv, send_sem=ns, recv_sem=nr, device_id=(send_to, m), device_id_type=MESH
+    )
+    beside.start()
+    own_cols = unpack([crv[p] for p in range(RANKS)], NB * OWN)
+    beside.wait_recv()
+    nb_cols = unpack([nrv[p] for p in range(RANKS)], NB * OWN)
+
+    def select(i, src):
+        cols = jnp.concatenate([own_cols[:, i * OWN : (i + 1) * OWN], nb_cols[:, i * OWN : (i + 1) * OWN]], axis=1)
+        at = lax.broadcasted_iota(jnp.int32, (2 * OWN, src.shape[1]), 0)
+        hot = jnp.where(at == src.astype(jnp.int32), 1.0, 0.0).astype(BF16)
+        got = jnp.dot(jnp.concatenate(list(split3(cols)), axis=0), hot, preferred_element_type=F32)
+        return got[:MEMBERS] + got[MEMBERS : 2 * MEMBERS] + got[2 * MEMBERS :]
+
+    n1 = INNER + OUTER
+    x1 = select(0, prm[3:4, :n1])
+    x2 = select(1, prm[3:4, n1:])
+    av, wv = stats(x1, prm[1:2, :n1], prm[2:3, :n1])
+    pv = column(prm[0:1, :n1])
+    a1[...] = av[:INNER]
+    w1[...] = wv[:, :INNER]
+    p1[...] = pv[:INNER]
+    x2 = update(x2, prm[0:1, n1:], pv, av, wv)
+    av, wv = stats(x2, prm[1:2, n1:], prm[2:3, n1:])
+    a2[...] = av
+    w2[...] = wv
+    p2[...] = column(prm[0:1, n1:])
+
+    first = (s * RANKS + m) * SUB
+
+    def back(d, c):
+        return pltpu.make_async_remote_copy(
+            src_ref=rpk.at[lax.rem(m + d, RANKS), c],
+            dst_ref=orv.at[m, c],
+            send_sem=bs.at[d - 1, c],
+            recv_sem=br.at[d - 1, c],
+            device_id=(s, lax.rem(m + d, RANKS)),
+            device_id_type=MESH,
+        )
+
+    def back_landed(d, c):
+        return pltpu.make_async_remote_copy(
+            src_ref=rpk.at[lax.rem(m + d, RANKS), c],
+            dst_ref=orv.at[lax.rem(m + RANKS - d, RANKS), c],
+            send_sem=bs.at[d - 1, c],
+            recv_sem=br.at[d - 1, c],
+            device_id=(s, lax.rem(m + d, RANKS)),
+            device_id_type=MESH,
+        )
+
+    def empty(ref, base):
+        half = CH // 2
+        out[0:8, pl.ds(base, CH)] = ref[:, 0:CH]
+        out[8:16, pl.ds(base, CH)] = ref[:, CH : 2 * CH]
+        out[16:20, pl.ds(base, half)] = ref[0:4, 2 * CH : PW]
+        out[16:20, pl.ds(base + half, half)] = ref[4:8, 2 * CH : PW]
+
+    def work(c, _):
+        for d in (1, 3, 2):
+            landed(d, c).wait_recv()
+        e = unpack([rv[p, c] for p in range(RANKS)], CH)
+        where = first + c * CH + lax.broadcasted_iota(jnp.int32, (1, CH), 1)
+        pos = where.astype(F32) * (1.0 / LOC_C)
+        e = update(e, pos, p1[...], a1[...], w1[...])
+        e = update(e, pos, p2[...], a2[...], w2[...])
+        for p, tiles in enumerate(pack(e)):
+            for begin, tile in tiles:
+                rpk[p, c, :, begin : begin + tile.shape[1]] = tile
+        for d in (1, 3, 2):
+            back(d, c).start()
+        empty(rpk.at[m, c], pl.multiple_of(m * SUB + c * CH, CH))
+        return 0
+
+    lax.fori_loop(0, NC, work, 0)
+
+    def finish(c, _):
+        for d in (1, 3, 2):
+            back_landed(d, c).wait_recv()
+            p = lax.rem(m + RANKS - d, RANKS)
+            empty(orv.at[p, c], pl.multiple_of(p * SUB + c * CH, CH))
+        return 0
+
+    lax.fori_loop(0, NC, finish, 0)
+
+    def drain(c, _):
+        for d in (1, 3, 2):
+            forward(d, c).wait_send()
+            back(d, c).wait_send()
+        return 0
+
+    lax.fori_loop(0, NC, drain, 0)
+    for d in (1, 3, 2):
+        columns(d).wait_send()
+    beside.wait_send()
+
+
+def fused(mesh, ensemble, offs, prm):
+    vm = pl.BlockSpec(memory_space=pltpu.VMEM)
+    n1 = INNER + OUTER
+    dma = pltpu.SemaphoreType.DMA
+    kd = MEMBERS // RANKS
+    return pl.pallas_call(
+        functools.partial(fused_kernel, mesh.shape["slab"]),
+        out_shape=jax.ShapeDtypeStruct((kd, SLAB), F32),
+        in_specs=[pl.BlockSpec(memory_space=pltpu.SMEM), vm, vm],
+        out_specs=vm,
+        scratch_shapes=[
+            pltpu.VMEM((SLAB // 128, kd, 128), F32),
+            pltpu.VMEM((RANKS - 1, NC, 8, PW), F32),
+            pltpu.VMEM((RANKS, NC, 8, PW), F32),
+            pltpu.VMEM((RANKS, NC, 8, PW), F32),
+            pltpu.VMEM((RANKS, NC, 8, PW), F32),
+            pltpu.VMEM((8, CW), F32),
+            pltpu.VMEM((RANKS, 8, CW), F32),
+            pltpu.VMEM((RANKS, 8, CW), F32),
+            pltpu.VMEM((INNER, 3 * MEMBERS), BF16),
+            pltpu.VMEM((2 * MEMBERS, INNER), BF16),
+            pltpu.VMEM((INNER, 128), F32),
+            pltpu.VMEM((INNER, 3 * MEMBERS), BF16),
+            pltpu.VMEM((2 * MEMBERS, INNER), BF16),
+            pltpu.VMEM((INNER, 128), F32),
+            dma((RANKS - 1, NC)),
+            dma((RANKS - 1, NC)),
+            dma((RANKS - 1, NC)),
+            dma((RANKS - 1, NC)),
+            dma((RANKS - 1,)),
+            dma((RANKS - 1,)),
+            dma,
+            dma,
+        ],
+        compiler_params=pltpu.CompilerParams(
+            collective_id=0, has_side_effects=True, vmem_limit_bytes=48 << 20
+        ),
+        name="fused",
+    )(offs, prm, ensemble)
+
+
+def local(mesh, ensemble, obs_value, obs_var, obs_slab, obs_offset, batch_order):
+    offs, prm, bad = prep(mesh, obs_value, obs_var, obs_slab, obs_offset, batch_order)
+    fits = jnp.max(bad) < 0.5
+    return lax.cond(
+        fits,
+        lambda: fused(mesh, ensemble, offs, prm),
+        lambda: general(ensemble, obs_value, obs_var, obs_slab, obs_offset, batch_order),
+    )
+
+
 def solution(mesh):
     return jax.shard_map(
-        local,
+        functools.partial(local, mesh),
         mesh=mesh,
         in_specs=(P("mem", "slab"), P(), P(), P(), P(), P()),
         out_specs=P("mem", "slab"),

time: 474 us -> 48.3 us (0.10)
  matrix products: 296 us -> 0 us
  local copies, waits for them, and re-layouts: 67.3 us -> 1.15 us
  Pallas kernels: 0 us -> 45.5 us
  other arithmetic: 31.3 us -> 0.6 us
  waiting for transfers between devices: 28.4 us -> 0 us
  blocking collectives: 21.3 us -> 0 us
  starting transfers between devices: 20.3 us -> 0 us
    dot_general x48 -> x0, matrix products: 296 us -> none  [the longest x16 172 us: add_block(): jnp.einsum('kv,ko->vo', state_anom, anom_blk, precision=lax.Precision.HIG...]
    pallas_call x0 -> x2, Pallas kernels: none -> 45.5 us  [the longest x1 41.9 us: fused(): pl.pallas_call(functools.partial(fused_kernel, mesh.shape['slab']), out_s...]
    all_to_all x1 -> x0, blocking collectives: 21.3 us -> none  [local(): lax.all_to_all(members, 'mem', split_axis=0, concat_axis=1, tiled=True)]
    reduce_sum x6 -> x0, other arithmetic: 16.5 us -> none  [the longest x2 6.7 us: local(): spread = jnp.sum(obs_anom * obs_anom, axis=0) / (total_members - 1.0)]
    gather x2 -> x0, local copies, waits for them, and re-layouts: 15.2 us -> none  [pick_columns(): jnp.take(members, safe_cols, axis=1) * usable.astype(jnp.float32)[None, :]]
    all_to_all x1 -> x0, waiting for transfers between devices: 14.6 us -> none  [local(): lax.all_to_all(ensemble, 'mem', split_axis=1, concat_axis=0, tiled=True)]
    ppermute x4 -> x0, starting transfers between devices: 14.5 us -> none  [from_behind(): lax.ppermute(value, axis, [(source, source + steps) for source in range(l...]
    ppermute x4 -> x0, waiting for transfers between devices: 13.9 us -> none  [from_behind(): lax.ppermute(value, axis, [(source, source + steps) for source in range(l...]
  transfers between devices with their start and end apart: 5 -> 0, of which waited for: 5 -> 0; matrix products, arithmetic and copies ran while one was open for 4% -> 0% of each run, Pallas kernels for 0% -> 0%
where the time goes in v1:
time: 48.3 us; the launch traced here: 48.1 us
  Pallas kernels  45.5 us (94%)
  local copies, waits for them, and re-layouts  1.15 us (2%)
  between operations  0.66 us (1%)
  other arithmetic  0.6 us (1%)
    pallas_call x1, Pallas kernels, fused(): pl.pallas_call(functools.partial(fused_kernel, mesh.shape['slab']), out_s...  41.9 us
    pallas_call x1, Pallas kernels, prep(): pl.pallas_call(functools.partial(prep_kernel, mesh.shape['slab']), out_sh...  3.57 us
    unnamed x1, local copies, waits for them, and re-layouts  1.15 us

profile of v1, /device:TPU:1, one launch (start us, length us, event | category | flops | bytes accessed | tf_op | source)
XLA Modules:
  0.0 48.1 jit_solution(10701339975918346049)
XLA Ops:
  0.0 3.6 %prep.1 = (s32[1,512]{1,0:T(1,128)}, f32[8,640]{1,0:T(8,128)}, f32[8,128]{1,0:T(8,128)S(1)}) custom-call(s32[2]{0:T(128)} %order.1, f32[2,2048]{1,0:T(2,128)} %val.1, f32[2,2048]{1,0:T(2,128)} %var.1, s32[2,2048]{1,0:T(2,128)} %slab.1, s32[2,2048]{1,0:T(2,128)} %off.1), custom_call_target="tpu_custom_call" | custom-call | tf_op jit(solution)/shard_map/prep/pallas_call | solution.py:203
  3.6 0.6 %reduce_max.9 = f32[]{:T(128)} reduce(f32[8,128]{1,0:T(8,128)S(1)} %get-tuple-element.533, f32[]{:T(128)} %constant.388.clone.1), dimensions={0,1}, to_apply=%region_0.0 | reduce | flops 1023 | bytes 4104 | tf_op jit(solution)/shard_map/reduce_max | solution.py:530
  4.8 42.2 %conditional.1 = (f32[20,16384]{1,0:T(8,128)S(1)}) conditional(s32[]{:T(128)} %convert_element_type.22, (f32[20,16384]{1,0:T(8,128)}, s32[2]{0:T(128)}, s32[2,2048]{1,0:T(2,128)}, s32[2,2048]{1,0:T(2,128)}, f32[2,2048]{1,0:T(2,128)}, /*index=5*/f32[2,2048]{1,0:T(2,128)}) %tuple.56, (s32[1,512]{1,0:T(1,128)}, f32[8,640]{1,0:T(8,128)}, ...), branch_computations={%region_1.13_spmd, %region_12.14_spmd} | conditional | flops 4132327424 | bytes 175662432 | solution.py:531
  5.1 41.9 %fused.1 = f32[20,16384]{1,0:T(8,128)S(1)} custom-call(s32[1,512]{1,0:T(1,128)} %get-tuple-element.527.offs, f32[8,640]{1,0:T(8,128)} %get-tuple-element.528.prm, f32[20,16384]{1,0:T(8,128)} %get-tuple-element.529.x), custom_call_target="tpu_custom_call" | custom-call | tf_op jit(solution)/shard_map/cond/branch_1_fun/fused/pallas_call | solution.py:492
  47.0 1.1 %copy.79 = f32[20,16384]{1,0:T(8,128)} copy(f32[20,16384]{1,0:T(8,128)S(1)} %get-tuple-element.536) | data formatting | bytes 2621440

commit v2 on v1

--- a/solution.py
+++ b/solution.py
@@ -16,6 +16,7 @@
 RANKS = 4
 SLAB = SUB * RANKS
 OBS = 2048
+SUB_BITS = 12
 OWN = 256
 INNER = 256
 OUTER = 128
@@ -121,104 +122,48 @@
     return a, b, c
 
 
-def prep_kernel(slabs, order, val, var, slab, off, offs_out, prm_out, ok_out):
-    s = lax.axis_index("slab")
-    m = lax.axis_index("mem")
-    first = (s * RANKS + m) * SUB
-    nb = lax.rem(s + jnp.where(m < RANKS // 2, slabs - 1, 1), slabs)
-    lane = lax.broadcasted_iota(jnp.int32, (8, OBS), 1)
-    rows = [pl.ds(order[i], 1) for i in range(NB)]
-    slab_b = [slab[r, :] for r in rows]
-    off_b = [off[r, :] for r in rows]
-    loc_b = [a * SLAB + b for a, b in zip(slab_b, off_b)]
-    rel_b = [a - first for a in loc_b]
-    own_b = [a == s for a in slab_b]
-    nb_b = [a == nb for a in slab_b]
-    inner_b = [(r >= -SUB) & (r < 2 * SUB) for r in rel_b]
-    outer = (rel_b[0] >= -2 * SUB) & (rel_b[0] < 3 * SUB) & jnp.logical_not(inner_b[0])
-    masks = own_b + nb_b + inner_b + [outer, outer]
-    marks = jnp.concatenate([jnp.where(a, 1, 0) for a in masks], axis=0)
+def prefix(marks):
+    lane = lax.broadcasted_iota(jnp.int32, marks.shape, 1)
     run = marks
     step = 1
-    while step < OBS:
+    while step < marks.shape[1]:
         run = run + jnp.where(lane >= step, pltpu.roll(run, step, 1), 0)
         step *= 2
-    run = run - marks
-    own_slot = [jnp.where(own_b[i], run[i : i + 1], -1) for i in range(NB)]
-    src = [jnp.where(own_b[i], run[i : i + 1], OWN + run[2 + i : 3 + i]) for i in range(NB)]
-    slot = [
-        jnp.where(inner_b[0], run[4:5], jnp.where(outer, INNER + run[6:7], -1)),
-        jnp.where(inner_b[1], run[5:6], -1),
-    ]
-    width = [INNER + OUTER, INNER]
-    begin = 0
-    for i in range(NB):
-        vals = jnp.concatenate(
-            [
-                loc_b[i].astype(F32) * (1.0 / LOC_C),
-                val[rows[i], :],
-                var[rows[i], :],
-                src[i].astype(F32),
-                jnp.ones((1, OBS), F32),
-                off_b[i].astype(F32),
-                jnp.zeros((2, OBS), F32),
-            ],
-            axis=0,
-        )
-        pieces = jnp.concatenate(list(split3(vals)), axis=0)
-        which = lax.broadcasted_iota(jnp.int32, (width[i], OBS), 0)
-        hot_w = jnp.where(which == slot[i], 1.0, 0.0).astype(BF16)
-        which_o = lax.broadcasted_iota(jnp.int32, (OWN, OBS), 0)
-        hot_o = jnp.where(which_o == own_slot[i], 1.0, 0.0).astype(BF16)
-        hot = jnp.concatenate([hot_w, hot_o], axis=0)
-        got = lax.dot_general(pieces, hot, (((1,), (1,)), ((), ())), preferred_element_type=F32)
-        got = got[0:8] + got[8:16] + got[16:24]
-        w = width[i]
-        there = got[4:5, :w] > 0.5
-        prm_out[0:1, begin : begin + w] = jnp.where(there, got[0:1, :w], FAR)
-        prm_out[1:2, begin : begin + w] = got[1:2, :w]
-        prm_out[2:3, begin : begin + w] = jnp.where(there, got[2:3, :w], 1.0)
-        prm_out[3:4, begin : begin + w] = jnp.where(there, got[3:4, :w], -1.0)
-        prm_out[4:8, begin : begin + w] = jnp.zeros((4, w), F32)
-        offs_out[0:1, i * OWN : (i + 1) * OWN] = got[5:6, w:].astype(jnp.int32)
-        begin += w
+    return run - marks
+
+
+def pull(pieces, slot, width):
+    at = lax.broadcasted_iota(jnp.int32, (width, OBS), 0)
+    hot = jnp.where(at == slot, 1.0, 0.0).astype(BF16)
+    got = lax.dot_general(pieces, hot, (((1,), (1,)), ((), ())), preferred_element_type=F32)
+    rows = pieces.shape[0] // 3
+    return got[:rows] + got[rows : 2 * rows] + got[2 * rows :]
+
+
+def count_over(loc_b):
     bad = jnp.zeros((8, 128), F32)
     bins = lax.broadcasted_iota(jnp.int32, (128, OBS), 0)
     at = lax.broadcasted_iota(jnp.int32, (8, 128), 1)
-    for i in range(NB):
-        hot = jnp.where(bins == loc_b[i] // SUB, 1.0, 0.0).astype(BF16)
+    for loc in loc_b:
+        hot = jnp.where(bins == lax.shift_right_logical(loc, SUB_BITS), 1.0, 0.0).astype(BF16)
         cnt = lax.dot_general(
             jnp.ones((8, OBS), BF16), hot, (((1,), (1,)), ((), ())), preferred_element_type=F32
         )
         around = [pltpu.roll(cnt, sh, 1) for sh in (1, 127, 2, 126, 3)]
         near = cnt + around[0] + around[1]
         far = around[2] + around[3]
-        whole = jnp.where(lax.rem(at, RANKS) == RANKS - 1, cnt + around[0] + around[2] + around[4], 0.0)
+        whole = jnp.where((at & (RANKS - 1)) == RANKS - 1, cnt + around[0] + around[2] + around[4], 0.0)
         bad = jnp.maximum(bad, jnp.where((near > INNER) | (far > OUTER) | (whole > OWN), 1.0, 0.0))
-    ok_out[...] = bad
-
-
-def prep(mesh, obs_value, obs_var, obs_slab, obs_offset, batch_order):
-    vm = pl.BlockSpec(memory_space=pltpu.VMEM)
-    return pl.pallas_call(
-        functools.partial(prep_kernel, mesh.shape["slab"]),
-        out_shape=(
-            jax.ShapeDtypeStruct((1, NB * OWN), jnp.int32),
-            jax.ShapeDtypeStruct((8, 2 * INNER + OUTER), F32),
-            jax.ShapeDtypeStruct((8, 128), F32),
-        ),
-        in_specs=[pl.BlockSpec(memory_space=pltpu.SMEM), vm, vm, vm, vm],
-        out_specs=(vm, vm, vm),
-        compiler_params=pltpu.CompilerParams(vmem_limit_bytes=48 << 20),
-        name="prep",
-    )(batch_order, obs_value, obs_var, obs_slab, obs_offset)
+    return jnp.max(bad)
 
 
 def taper(z):
     p_in = (((-0.25 * z + 0.5) * z + 0.625) * z - 5.0 / 3.0) * (z * z) + 1.0
     t = jnp.maximum(2.0 - z, 0.0)
     t = t * t
-    p_out = (t * t) * ((z * (1.0 / 12.0) + 1.0 / 6.0) - (1.0 / 24.0) / jnp.maximum(z, 1.0))
+    r = pl.reciprocal(z, approx=True)
+    r = r * (1.0 / 12.0 - (1.0 / 24.0) * z * r)
+    p_out = (t * t) * ((z * (1.0 / 12.0) + 1.0 / 6.0) - r)
     return jnp.where(z <= 1.0, p_in, p_out)
 
 
@@ -285,20 +230,23 @@
 
 
 def fused_kernel(
-    slabs, offs, prm, x, out,
-    xb, pk, rv, rpk, orv, cpk, crv, nrv, a1, w1, p1, a2, w2, p2,
-    fs, fr, bs, br, cs, cr, ns, nr,
+    slabs, order, val, var, slab, off, x_hbm, out, bad,
+    x, pk, rv, rpk, cpk, crv, nrv, a1, w1, p1, a2, w2, p2,
+    xs, fs, fr, bs, br, ks, cs, cr, ns, nr,
 ):
     s = lax.axis_index("slab")
     m = lax.axis_index("mem")
     below = m < RANKS // 2
     send_to = lax.rem(s + jnp.where(below, 1, slabs - 1), slabs)
     gets_from = lax.rem(s + jnp.where(below, slabs - 1, 1), slabs)
+    load = pltpu.make_async_copy(x_hbm, x, xs)
+    load.start()
 
     barrier = pltpu.get_barrier_semaphore()
     for d in range(1, RANKS):
         pl.semaphore_signal(barrier, inc=1, device_id=(s, lax.rem(m + d, RANKS)), device_id_type=MESH)
     pl.semaphore_signal(barrier, inc=1, device_id=(gets_from, m), device_id_type=MESH)
+    load.wait()
     pl.semaphore_wait(barrier, RANKS)
 
     def fill(ref, base):
@@ -328,38 +276,90 @@
             device_id_type=MESH,
         )
 
-    def send_chunk(c, _):
+    def fill_chunk(c):
         for d in (1, 3, 2):
             p = lax.rem(m + d, RANKS)
             fill(pk.at[d - 1, c], pl.multiple_of(p * SUB + c * CH, CH))
+        fill(rv.at[m, c], pl.multiple_of(m * SUB + c * CH, CH))
+
+    def send_chunk(c):
+        for d in (1, 3, 2):
             forward(d, c).start()
-        fill(rv.at[m, c], pl.multiple_of(m * SUB + c * CH, CH))
+
+    def first_chunks(c, _):
+        fill_chunk(c)
+        send_chunk(c)
         return 0
 
-    lax.fori_loop(0, EARLY, send_chunk, 0)
-
-    def spread_out(i, _):
-        for k in range(8):
-            xb[i * 8 + k] = x[:, pl.ds(pl.multiple_of(i * 1024 + k * 128, 128), 128)]
+    def fill_later(c, _):
+        fill_chunk(c)
         return 0
 
-    lax.fori_loop(0, SLAB // 1024, spread_out, 0)
-    lane = lax.broadcasted_iota(jnp.int32, (20, 128), 1)
-    half = OWN
-    for t in range(NB * OWN // 128):
-
-        def pick(j, acc):
-            o = offs[0, t * 128 + j]
-            blk = xb[lax.shift_right_logical(o, 7)]
-            one = jnp.sum(jnp.where(lane == (o & 127), blk, 0.0), axis=1, keepdims=True)
-            return jnp.where(lane == j, one, acc)
-
-        cols = lax.fori_loop(0, 128, pick, jnp.zeros((20, 128), F32), unroll=8)
-        cpk[:, t * 128 : (t + 1) * 128] = cols[0:8]
-        cpk[:, NB * OWN + t * 128 : NB * OWN + (t + 1) * 128] = cols[8:16]
-        r = 0 if t * 128 < half else 4
-        q = 2 * NB * OWN + (t * 128) % half
-        cpk[r : r + 4, q : q + 128] = cols[16:20]
+    def send_later(c, _):
+        send_chunk(c)
+        return 0
+
+    lax.fori_loop(0, EARLY, first_chunks, 0)
+    lax.fori_loop(EARLY, NC, fill_later, 0)
+
+    first = (s * RANKS + m) * SUB
+    rows = [pl.ds(order[i], 1) for i in range(NB)]
+    slab_b = [slab[r, :] for r in rows]
+    off_b = [off[r, :] for r in rows]
+    loc_b = [a * SLAB + b for a, b in zip(slab_b, off_b)]
+    rel_b = [a - first for a in loc_b]
+    own_b = [a == s for a in slab_b]
+    nb_b = [a == gets_from for a in slab_b]
+    inner_b = [(r >= -SUB) & (r < 2 * SUB) for r in rel_b]
+    outer = (rel_b[0] >= -2 * SUB) & (rel_b[0] < 3 * SUB) & jnp.logical_not(inner_b[0])
+    masks = own_b + nb_b + inner_b + [outer, outer]
+    run = prefix(jnp.concatenate([jnp.where(a, 1, 0) for a in masks], axis=0))
+
+    offs = []
+    for i in range(NB):
+        tile = lax.shift_right_logical(off_b[i], 7).astype(F32)
+        lane = (off_b[i] & 127).astype(F32)
+        at = lax.broadcasted_iota(jnp.int32, (OWN, OBS), 0)
+        hot = jnp.where(at == jnp.where(own_b[i], run[i : i + 1], -1), 1.0, 0.0).astype(BF16)
+        both = jnp.concatenate([tile, lane, jnp.zeros((6, OBS), F32)], axis=0).astype(BF16)
+        offs.append(lax.dot_general(both, hot, (((1,), (1,)), ((), ())), preferred_element_type=F32))
+    offs = jnp.concatenate(offs, axis=1).astype(jnp.int32)
+    n = NB * OWN
+    at = lax.broadcasted_iota(jnp.int32, (128, n), 0)
+    hot = jnp.where(at == offs[1:2], 1.0, 0.0).astype(BF16)
+    hot = jnp.concatenate([hot, hot], axis=0)
+    low = lax.broadcasted_iota(jnp.int32, (8, n), 0) < 4
+    tile = jnp.broadcast_to(offs[0:1], (8, n))
+    tile_tail = tile - jnp.where(low, 0, CH // 256)
+    per = CH // 128
+
+    def pick(ref, base, acc):
+        one, two, tail = acc
+        t = jnp.concatenate([ref[:, k * 128 : (k + 1) * 128] for k in range(PW // 128)], axis=0)
+        hi = t.astype(BF16)
+        mid = (t - hi.astype(F32)).astype(BF16)
+        y = jnp.dot(jnp.concatenate([hi, mid], axis=1), hot, preferred_element_type=F32)
+        for k in range(per):
+            here = tile == base + k
+            one = jnp.where(here, y[8 * k : 8 * k + 8], one)
+            two = jnp.where(here, y[8 * (per + k) : 8 * (per + k) + 8], two)
+        for k in range(per // 2):
+            q = 8 * (2 * per + k)
+            tail = jnp.where(tile_tail == base + k, y[q : q + 8], tail)
+        return one, two, tail
+
+    def pick_chunk(c, acc):
+        acc = pick(rv.at[m, c], m * (SUB // 128) + c * per, acc)
+        for d in (1, 3, 2):
+            acc = pick(pk.at[d - 1, c], lax.rem(m + d, RANKS) * (SUB // 128) + c * per, acc)
+        return acc
+
+    none = jnp.zeros((8, n), F32)
+    one, two, tail = lax.fori_loop(0, NC, pick_chunk, (none, none, none))
+    tail = tail + pltpu.roll(tail, 4, 0)
+    cpk[:, 0:n] = one
+    cpk[:, n : 2 * n] = two
+    cpk[:, 2 * n : CW] = jnp.where(low[:, : n // 2], tail[:, : n // 2], tail[:, n // 2 :])
 
     def columns(d):
         return pltpu.make_async_remote_copy(
@@ -384,7 +384,36 @@
     for d in (1, 3, 2):
         columns(d).start()
     crv[m] = cpk[...]
-    lax.fori_loop(EARLY, NC, send_chunk, 0)
+    lax.fori_loop(EARLY, NC, send_later, 0)
+
+    prm = []
+    for i in range(NB):
+        src = jnp.where(own_b[i], run[i : i + 1], OWN + run[2 + i : 3 + i])
+        slot = jnp.where(inner_b[i], run[4 + i : 5 + i], -1)
+        if i == 0:
+            slot = jnp.where(outer, INNER + run[6:7], slot)
+        vals = jnp.concatenate(
+            [
+                loc_b[i].astype(F32) * (1.0 / LOC_C),
+                val[rows[i], :],
+                var[rows[i], :],
+                src.astype(F32),
+                jnp.ones((1, OBS), F32),
+                jnp.zeros((3, OBS), F32),
+            ],
+            axis=0,
+        )
+        got = pull(jnp.concatenate(list(split3(vals)), axis=0), slot, INNER + (OUTER if i == 0 else 0))
+        there = got[4:5] > 0.5
+        prm.append(
+            (
+                jnp.where(there, got[0:1], FAR),
+                got[1:2],
+                jnp.where(there, got[2:3], 1.0),
+                jnp.where(there, got[3:4], -1.0),
+            )
+        )
+    bad[0] = count_over(loc_b)
     for d in (1, 3, 2):
         columns_landed(d).wait_recv()
     beside = pltpu.make_async_remote_copy(
@@ -402,26 +431,23 @@
         got = jnp.dot(jnp.concatenate(list(split3(cols)), axis=0), hot, preferred_element_type=F32)
         return got[:MEMBERS] + got[MEMBERS : 2 * MEMBERS] + got[2 * MEMBERS :]
 
-    n1 = INNER + OUTER
-    x1 = select(0, prm[3:4, :n1])
-    x2 = select(1, prm[3:4, n1:])
-    av, wv = stats(x1, prm[1:2, :n1], prm[2:3, :n1])
-    pv = column(prm[0:1, :n1])
+    x1 = select(0, prm[0][3])
+    x2 = select(1, prm[1][3])
+    av, wv = stats(x1, prm[0][1], prm[0][2])
+    pv = column(prm[0][0])
     a1[...] = av[:INNER]
     w1[...] = wv[:, :INNER]
     p1[...] = pv[:INNER]
-    x2 = update(x2, prm[0:1, n1:], pv, av, wv)
-    av, wv = stats(x2, prm[1:2, n1:], prm[2:3, n1:])
+    x2 = update(x2, prm[1][0], pv, av, wv)
+    av, wv = stats(x2, prm[1][1], prm[1][2])
     a2[...] = av
     w2[...] = wv
-    p2[...] = column(prm[0:1, n1:])
-
-    first = (s * RANKS + m) * SUB
+    p2[...] = column(prm[1][0])
 
     def back(d, c):
         return pltpu.make_async_remote_copy(
             src_ref=rpk.at[lax.rem(m + d, RANKS), c],
-            dst_ref=orv.at[m, c],
+            dst_ref=out.at[m, c],
             send_sem=bs.at[d - 1, c],
             recv_sem=br.at[d - 1, c],
             device_id=(s, lax.rem(m + d, RANKS)),
@@ -431,19 +457,15 @@
     def back_landed(d, c):
         return pltpu.make_async_remote_copy(
             src_ref=rpk.at[lax.rem(m + d, RANKS), c],
-            dst_ref=orv.at[lax.rem(m + RANKS - d, RANKS), c],
+            dst_ref=out.at[lax.rem(m + RANKS - d, RANKS), c],
             send_sem=bs.at[d - 1, c],
             recv_sem=br.at[d - 1, c],
             device_id=(s, lax.rem(m + d, RANKS)),
             device_id_type=MESH,
         )
 
-    def empty(ref, base):
-        half = CH // 2
-        out[0:8, pl.ds(base, CH)] = ref[:, 0:CH]
-        out[8:16, pl.ds(base, CH)] = ref[:, CH : 2 * CH]
-        out[16:20, pl.ds(base, half)] = ref[0:4, 2 * CH : PW]
-        out[16:20, pl.ds(base + half, half)] = ref[4:8, 2 * CH : PW]
+    def keep(c):
+        return pltpu.make_async_copy(rpk.at[m, c], out.at[m, c], ks.at[c])
 
     def work(c, _):
         for d in (1, 3, 2):
@@ -458,46 +480,41 @@
                 rpk[p, c, :, begin : begin + tile.shape[1]] = tile
         for d in (1, 3, 2):
             back(d, c).start()
-        empty(rpk.at[m, c], pl.multiple_of(m * SUB + c * CH, CH))
+        keep(c).start()
         return 0
 
     lax.fori_loop(0, NC, work, 0)
 
     def finish(c, _):
-        for d in (1, 3, 2):
-            back_landed(d, c).wait_recv()
-            p = lax.rem(m + RANKS - d, RANKS)
-            empty(orv.at[p, c], pl.multiple_of(p * SUB + c * CH, CH))
-        return 0
-
-    lax.fori_loop(0, NC, finish, 0)
-
-    def drain(c, _):
         for d in (1, 3, 2):
             forward(d, c).wait_send()
             back(d, c).wait_send()
+            back_landed(d, c).wait_recv()
+        keep(c).wait()
         return 0
 
-    lax.fori_loop(0, NC, drain, 0)
+    lax.fori_loop(0, NC, finish, 0)
     for d in (1, 3, 2):
         columns(d).wait_send()
     beside.wait_send()
 
 
-def fused(mesh, ensemble, offs, prm):
+def fused(mesh, ensemble, obs_value, obs_var, obs_slab, obs_offset, batch_order):
     vm = pl.BlockSpec(memory_space=pltpu.VMEM)
-    n1 = INNER + OUTER
+    sm = pl.BlockSpec(memory_space=pltpu.SMEM)
+    hbm = pl.BlockSpec(memory_space=pl.ANY)
     dma = pltpu.SemaphoreType.DMA
-    kd = MEMBERS // RANKS
     return pl.pallas_call(
         functools.partial(fused_kernel, mesh.shape["slab"]),
-        out_shape=jax.ShapeDtypeStruct((kd, SLAB), F32),
-        in_specs=[pl.BlockSpec(memory_space=pltpu.SMEM), vm, vm],
-        out_specs=vm,
+        out_shape=(
+            jax.ShapeDtypeStruct((RANKS, NC, 8, PW), F32),
+            jax.ShapeDtypeStruct((1,), F32),
+        ),
+        in_specs=[sm, vm, vm, vm, vm, hbm],
+        out_specs=(hbm, sm),
         scratch_shapes=[
-            pltpu.VMEM((SLAB // 128, kd, 128), F32),
+            pltpu.VMEM((MEMBERS // RANKS, SLAB), F32),
             pltpu.VMEM((RANKS - 1, NC, 8, PW), F32),
-            pltpu.VMEM((RANKS, NC, 8, PW), F32),
             pltpu.VMEM((RANKS, NC, 8, PW), F32),
             pltpu.VMEM((RANKS, NC, 8, PW), F32),
             pltpu.VMEM((8, CW), F32),
@@ -509,10 +526,12 @@
             pltpu.VMEM((INNER, 3 * MEMBERS), BF16),
             pltpu.VMEM((2 * MEMBERS, INNER), BF16),
             pltpu.VMEM((INNER, 128), F32),
+            dma,
             dma((RANKS - 1, NC)),
             dma((RANKS - 1, NC)),
             dma((RANKS - 1, NC)),
             dma((RANKS - 1, NC)),
+            dma((NC,)),
             dma((RANKS - 1,)),
             dma((RANKS - 1,)),
             dma,
@@ -522,17 +541,35 @@
             collective_id=0, has_side_effects=True, vmem_limit_bytes=48 << 20
         ),
         name="fused",
-    )(offs, prm, ensemble)
+    )(batch_order, obs_value, obs_var, obs_slab, obs_offset, ensemble)
+
+
+def lay_kernel(got, out):
+    half = CH // 2
+    for c in range(got.shape[1]):
+        base = c * CH
+        out[0:8, base : base + CH] = got[0, c, :, 0:CH]
+        out[8:16, base : base + CH] = got[0, c, :, CH : 2 * CH]
+        out[16:20, base : base + half] = got[0, c, 0:4, 2 * CH : PW]
+        out[16:20, base + half : base + CH] = got[0, c, 4:8, 2 * CH : PW]
+
+
+def lay(got):
+    parts = 2
+    return pl.pallas_call(
+        lay_kernel,
+        grid=(RANKS, parts),
+        out_shape=jax.ShapeDtypeStruct((MEMBERS // RANKS, SLAB), F32),
+        in_specs=[pl.BlockSpec((1, NC // parts, 8, PW), lambda p, h: (p, h, 0, 0))],
+        out_specs=pl.BlockSpec((MEMBERS // RANKS, SUB // parts), lambda p, h: (0, p * parts + h)),
+        name="lay",
+    )(got)
 
 
 def local(mesh, ensemble, obs_value, obs_var, obs_slab, obs_offset, batch_order):
-    offs, prm, bad = prep(mesh, obs_value, obs_var, obs_slab, obs_offset, batch_order)
-    fits = jnp.max(bad) < 0.5
-    return lax.cond(
-        fits,
-        lambda: fused(mesh, ensemble, offs, prm),
-        lambda: general(ensemble, obs_value, obs_var, obs_slab, obs_offset, batch_order),
-    )
+    args = (ensemble, obs_value, obs_var, obs_slab, obs_offset, batch_order)
+    got, bad = fused(mesh, *args)
+    return lax.cond(bad[0] < 0.5, lambda: lay(got), lambda: general(*args))
 
 
 def solution(mesh):

time: 48.3 us -> 48.5 us (level)
  Pallas kernels: 45.5 us -> 46.2 us
  other arithmetic: 0.6 us -> 0 us
    reduce_max x1 -> x0, other arithmetic: 0.6 us -> none  [local(): fits = jnp.max(bad) < 0.5]
    unnamed x1 -> x2, local copies, waits for them, and re-layouts: 1.15 us -> 1.14 us
where the time goes in v2:
time: 48.5 us; the launch traced here: 48.2 us
  Pallas kernels  46.2 us (95%)
  local copies, waits for them, and re-layouts  1.14 us (2%)
  between operations  0.65 us (1%)
    pallas_call x1, Pallas kernels, fused(): pl.pallas_call(functools.partial(fused_kernel, mesh.shape['slab']), out_s...  42.2 us
    pallas_call x1, Pallas kernels, lay(): pl.pallas_call(lay_kernel, grid=(RANKS, parts), out_shape=jax.ShapeDtypeS...  4.01 us
    unnamed x2, local copies, waits for them, and re-layouts  1.14 us

profile of v2, /device:TPU:1, one launch (start us, length us, event | category | flops | bytes accessed | tf_op | source)
XLA Modules:
  0.0 48.2 jit_solution(11046215744654867195)
XLA Ops:
  0.0 42.2 %fused.1 = (f32[4,8,8,1280]{3,2,1,0:T(8,128)}, f32[1]{0:T(128)}) custom-call(s32[2]{0:T(128)} %order.1, f32[2,2048]{1,0:T(2,128)} %val.1, f32[2,2048]{1,0:T(2,128)} %var.1, s32[2,2048]{1,0:T(2,128)} %slab.1, s32[2,2048]{1,0:T(2,128)} %off.1, f32[20,16384]{1,0:T(8,128)} %x_hbm.1), custom_call_target="tpu_custom_call" | custom-call | tf_op jit(solution)/shard_map/fused/pallas_call | solution.py:507
  42.8 4.2 %conditional.1 = (f32[20,16384]{1,0:T(8,128)S(1)}) conditional(s32[]{:T(128)} %bitcast.16, (f32[20,16384]{1,0:T(8,128)}, s32[2]{0:T(128)}, s32[2,2048]{1,0:T(2,128)}, s32[2,2048]{1,0:T(2,128)}, f32[2,2048]{1,0:T(2,128)}, /*index=5*/f32[2,2048]{1,0:T(2,128)}) %tuple.56, f32[4,8,8,1280]{3,2,1,0:T(8,128)} %get-tuple-element.525), branch_computations={%region_0.12_spmd, %region_11.13_spmd} | conditional | flops 4132327424 | bytes 175662432 | solution.py:572
  43.0 4.0 %lay.1 = f32[20,16384]{1,0:T(8,128)S(1)} custom-call(f32[4,8,8,1280]{3,2,1,0:T(8,128)} %got), custom_call_target="tpu_custom_call" | custom-call | tf_op jit(solution)/shard_map/cond/branch_1_fun/lay/pallas_call | solution.py:559
  47.0 0.0 copy-start.5
  47.0 1.1 %copy-done.5 = f32[20,16384]{1,0:T(8,128)} copy-done((f32[20,16384]{1,0:T(8,128)}, f32[20,16384]{1,0:T(8,128)S(1)}, u32[]{:S(2)}) %copy-start.5) | copy-done | bytes 1310744
Async XLA Ops:
  47.0 1.1 %copy-start.5 = (f32[20,16384]{1,0:T(8,128)}, f32[20,16384]{1,0:T(8,128)S(1)}, u32[]{:S(2)}) copy-start(f32[20,16384]{1,0:T(8,128)S(1)} %get-tuple-element.964) | copy-start | bytes 3932164

commit v3 on v2

--- a/solution.py
+++ b/solution.py
@@ -24,7 +24,9 @@
 NC = SUB // CH
 PW = CH * 5 // 2
 CW = 2 * OWN * 5 // 2
-EARLY = 4
+EARLY = 2
+MID = 4
+LAG = 4
 FAR = -1.0e5
 MESH = pl.DeviceIdType.MESH
 F32 = jnp.float32
@@ -123,13 +125,20 @@
 
 
 def prefix(marks):
-    lane = lax.broadcasted_iota(jnp.int32, marks.shape, 1)
-    run = marks
-    step = 1
-    while step < marks.shape[1]:
-        run = run + jnp.where(lane >= step, pltpu.roll(run, step, 1), 0)
-        step *= 2
-    return run - marks
+    blocks = OBS // 128
+    n = 8 * blocks
+    stack = jnp.concatenate([marks[:, b * 128 : (b + 1) * 128] for b in range(blocks)], axis=0).astype(BF16)
+    row = lax.broadcasted_iota(jnp.int32, (128, 128), 0)
+    col = lax.broadcasted_iota(jnp.int32, (128, 128), 1)
+    inside = jnp.dot(stack, jnp.where(row < col, 1.0, 0.0).astype(BF16), preferred_element_type=F32)
+    total = jnp.dot(stack, jnp.ones((128, 128), BF16), preferred_element_type=F32).astype(BF16)
+    row = lax.broadcasted_iota(jnp.int32, (n, n), 0)
+    col = lax.broadcasted_iota(jnp.int32, (n, n), 1)
+    same = (row & 7) == (col & 7)
+    earlier = lax.shift_right_logical(col, 3) < lax.shift_right_logical(row, 3)
+    before = jnp.dot(jnp.where(same & earlier, 1.0, 0.0).astype(BF16), total, preferred_element_type=F32)
+    run = (inside + before).astype(jnp.int32)
+    return jnp.concatenate([run[b * 8 : b * 8 + 8] for b in range(blocks)], axis=1)
 
 
 def pull(pieces, slot, width):
@@ -162,18 +171,18 @@
     t = jnp.maximum(2.0 - z, 0.0)
     t = t * t
     r = pl.reciprocal(z, approx=True)
-    r = r * (1.0 / 12.0 - (1.0 / 24.0) * z * r)
-    p_out = (t * t) * ((z * (1.0 / 12.0) + 1.0 / 6.0) - r)
+    p_out = (t * t) * ((z * (1.0 / 12.0) + 1.0 / 6.0) - r * (1.0 / 24.0))
     return jnp.where(z <= 1.0, p_in, p_out)
 
 
-def update(e, pos_v, pos_o, a, wst):
-    n = e.shape[1]
+def reach(pos_v, pos_o):
+    return taper(jnp.abs(pos_v - jnp.concatenate([pos_o] * (pos_v.shape[1] // 128), axis=1)))
+
+
+def update(e, rho, a, wst):
     eh = e.astype(BF16)
     el = (e - eh.astype(F32)).astype(BF16)
-    cov = jnp.dot(a, jnp.concatenate([eh, el, eh], axis=0), preferred_element_type=F32)
-    z = jnp.abs(pos_v - jnp.concatenate([pos_o] * (n // 128), axis=1))
-    g = taper(z) * cov
+    g = rho * jnp.dot(a, jnp.concatenate([eh, el, eh], axis=0), preferred_element_type=F32)
     gh = g.astype(BF16)
     gl = (g - gh.astype(F32)).astype(BF16)
     one = jnp.dot(wst, gh, preferred_element_type=F32)
@@ -230,9 +239,9 @@
 
 
 def fused_kernel(
-    slabs, order, val, var, slab, off, x_hbm, out, bad,
-    x, pk, rv, rpk, cpk, crv, nrv, a1, w1, p1, a2, w2, p2,
-    xs, fs, fr, bs, br, ks, cs, cr, ns, nr,
+    slabs, order, val, var, slab, off, x_hbm, out,
+    x, pk, rv, rpk, orv, cpk, crv, nrv, a1, w1, p1, r1, a2, w2, p2, r2,
+    xs, fs, fr, bs, br, cs, cr, ns, nr,
 ):
     s = lax.axis_index("slab")
     m = lax.axis_index("mem")
@@ -246,62 +255,6 @@
     for d in range(1, RANKS):
         pl.semaphore_signal(barrier, inc=1, device_id=(s, lax.rem(m + d, RANKS)), device_id_type=MESH)
     pl.semaphore_signal(barrier, inc=1, device_id=(gets_from, m), device_id_type=MESH)
-    load.wait()
-    pl.semaphore_wait(barrier, RANKS)
-
-    def fill(ref, base):
-        half = CH // 2
-        ref[:, 0:CH] = x[0:8, pl.ds(base, CH)]
-        ref[:, CH : 2 * CH] = x[8:16, pl.ds(base, CH)]
-        ref[0:4, 2 * CH : PW] = x[16:20, pl.ds(base, half)]
-        ref[4:8, 2 * CH : PW] = x[16:20, pl.ds(base + half, half)]
-
-    def forward(d, c):
-        return pltpu.make_async_remote_copy(
-            src_ref=pk.at[d - 1, c],
-            dst_ref=rv.at[m, c],
-            send_sem=fs.at[d - 1, c],
-            recv_sem=fr.at[d - 1, c],
-            device_id=(s, lax.rem(m + d, RANKS)),
-            device_id_type=MESH,
-        )
-
-    def landed(d, c):
-        return pltpu.make_async_remote_copy(
-            src_ref=pk.at[d - 1, c],
-            dst_ref=rv.at[lax.rem(m + RANKS - d, RANKS), c],
-            send_sem=fs.at[d - 1, c],
-            recv_sem=fr.at[d - 1, c],
-            device_id=(s, lax.rem(m + d, RANKS)),
-            device_id_type=MESH,
-        )
-
-    def fill_chunk(c):
-        for d in (1, 3, 2):
-            p = lax.rem(m + d, RANKS)
-            fill(pk.at[d - 1, c], pl.multiple_of(p * SUB + c * CH, CH))
-        fill(rv.at[m, c], pl.multiple_of(m * SUB + c * CH, CH))
-
-    def send_chunk(c):
-        for d in (1, 3, 2):
-            forward(d, c).start()
-
-    def first_chunks(c, _):
-        fill_chunk(c)
-        send_chunk(c)
-        return 0
-
-    def fill_later(c, _):
-        fill_chunk(c)
-        return 0
-
-    def send_later(c, _):
-        send_chunk(c)
-        return 0
-
-    lax.fori_loop(0, EARLY, first_chunks, 0)
-    lax.fori_loop(EARLY, NC, fill_later, 0)
-
     first = (s * RANKS + m) * SUB
     rows = [pl.ds(order[i], 1) for i in range(NB)]
     slab_b = [slab[r, :] for r in rows]
@@ -313,7 +266,7 @@
     inner_b = [(r >= -SUB) & (r < 2 * SUB) for r in rel_b]
     outer = (rel_b[0] >= -2 * SUB) & (rel_b[0] < 3 * SUB) & jnp.logical_not(inner_b[0])
     masks = own_b + nb_b + inner_b + [outer, outer]
-    run = prefix(jnp.concatenate([jnp.where(a, 1, 0) for a in masks], axis=0))
+    run = prefix(jnp.concatenate([jnp.where(a, 1.0, 0.0) for a in masks], axis=0))
 
     offs = []
     for i in range(NB):
@@ -324,6 +277,63 @@
         both = jnp.concatenate([tile, lane, jnp.zeros((6, OBS), F32)], axis=0).astype(BF16)
         offs.append(lax.dot_general(both, hot, (((1,), (1,)), ((), ())), preferred_element_type=F32))
     offs = jnp.concatenate(offs, axis=1).astype(jnp.int32)
+
+    load.wait()
+    pl.semaphore_wait(barrier, RANKS)
+
+    def fill(ref, base):
+        half = CH // 2
+        ref[:, 0:CH] = x[0:8, pl.ds(base, CH)]
+        ref[:, CH : 2 * CH] = x[8:16, pl.ds(base, CH)]
+        ref[0:4, 2 * CH : PW] = x[16:20, pl.ds(base, half)]
+        ref[4:8, 2 * CH : PW] = x[16:20, pl.ds(base + half, half)]
+
+    def forward(d, c):
+        return pltpu.make_async_remote_copy(
+            src_ref=pk.at[d - 1, c],
+            dst_ref=rv.at[m, c],
+            send_sem=fs.at[d - 1, c],
+            recv_sem=fr.at[d - 1, c],
+            device_id=(s, lax.rem(m + d, RANKS)),
+            device_id_type=MESH,
+        )
+
+    def landed(d, c):
+        return pltpu.make_async_remote_copy(
+            src_ref=pk.at[d - 1, c],
+            dst_ref=rv.at[lax.rem(m + RANKS - d, RANKS), c],
+            send_sem=fs.at[d - 1, c],
+            recv_sem=fr.at[d - 1, c],
+            device_id=(s, lax.rem(m + d, RANKS)),
+            device_id_type=MESH,
+        )
+
+    def fill_chunk(c):
+        for d in (1, 3, 2):
+            p = lax.rem(m + d, RANKS)
+            fill(pk.at[d - 1, c], pl.multiple_of(p * SUB + c * CH, CH))
+        fill(rv.at[m, c], pl.multiple_of(m * SUB + c * CH, CH))
+
+    def send_chunk(c):
+        for d in (1, 3, 2):
+            forward(d, c).start()
+
+    def first_chunks(c, _):
+        fill_chunk(c)
+        send_chunk(c)
+        return 0
+
+    def fill_later(c, _):
+        fill_chunk(c)
+        return 0
+
+    def send_later(c, _):
+        send_chunk(c)
+        return 0
+
+    lax.fori_loop(0, EARLY, first_chunks, 0)
+    lax.fori_loop(EARLY, NC, fill_later, 0)
+
     n = NB * OWN
     at = lax.broadcasted_iota(jnp.int32, (128, n), 0)
     hot = jnp.where(at == offs[1:2], 1.0, 0.0).astype(BF16)
@@ -384,7 +394,7 @@
     for d in (1, 3, 2):
         columns(d).start()
     crv[m] = cpk[...]
-    lax.fori_loop(EARLY, NC, send_later, 0)
+    lax.fori_loop(EARLY, MID, send_later, 0)
 
     prm = []
     for i in range(NB):
@@ -413,13 +423,27 @@
                 jnp.where(there, got[3:4], -1.0),
             )
         )
-    bad[0] = count_over(loc_b)
+    here = (first + lax.broadcasted_iota(jnp.int32, (1, CH), 1)).astype(F32) * (1.0 / LOC_C)
+    pv = column(prm[0][0])
+    p1[...] = pv[:INNER]
+    p2[...] = column(prm[1][0])
+
+    def tapers(dst, src):
+        def step(c, _):
+            dst[c] = reach(here + c.astype(F32) * (CH / LOC_C), src[...])
+            return 0
+
+        lax.fori_loop(0, NC, step, 0)
+
+    tapers(r1, p1)
     for d in (1, 3, 2):
         columns_landed(d).wait_recv()
     beside = pltpu.make_async_remote_copy(
         src_ref=crv, dst_ref=nrv, send_sem=ns, recv_sem=nr, device_id=(send_to, m), device_id_type=MESH
     )
     beside.start()
+    lax.fori_loop(MID, NC, send_later, 0)
+    tapers(r2, p2)
     own_cols = unpack([crv[p] for p in range(RANKS)], NB * OWN)
     beside.wait_recv()
     nb_cols = unpack([nrv[p] for p in range(RANKS)], NB * OWN)
@@ -434,20 +458,17 @@
     x1 = select(0, prm[0][3])
     x2 = select(1, prm[1][3])
     av, wv = stats(x1, prm[0][1], prm[0][2])
-    pv = column(prm[0][0])
     a1[...] = av[:INNER]
     w1[...] = wv[:, :INNER]
-    p1[...] = pv[:INNER]
-    x2 = update(x2, prm[1][0], pv, av, wv)
+    x2 = update(x2, reach(prm[1][0], pv), av, wv)
     av, wv = stats(x2, prm[1][1], prm[1][2])
     a2[...] = av
     w2[...] = wv
-    p2[...] = column(prm[1][0])
 
     def back(d, c):
         return pltpu.make_async_remote_copy(
             src_ref=rpk.at[lax.rem(m + d, RANKS), c],
-            dst_ref=out.at[m, c],
+            dst_ref=orv.at[m, c],
             send_sem=bs.at[d - 1, c],
             recv_sem=br.at[d - 1, c],
             device_id=(s, lax.rem(m + d, RANKS)),
@@ -457,40 +478,60 @@
     def back_landed(d, c):
         return pltpu.make_async_remote_copy(
             src_ref=rpk.at[lax.rem(m + d, RANKS), c],
-            dst_ref=out.at[lax.rem(m + RANKS - d, RANKS), c],
+            dst_ref=orv.at[lax.rem(m + RANKS - d, RANKS), c],
             send_sem=bs.at[d - 1, c],
             recv_sem=br.at[d - 1, c],
             device_id=(s, lax.rem(m + d, RANKS)),
             device_id_type=MESH,
         )
 
-    def keep(c):
-        return pltpu.make_async_copy(rpk.at[m, c], out.at[m, c], ks.at[c])
-
-    def work(c, _):
+    def place(ref, d, c):
+        base = pl.multiple_of(lax.rem(m + RANKS - d, RANKS) * SUB + c * CH, CH)
+        half = CH // 2
+        out[0:8, pl.ds(base, CH)] = ref[:, 0:CH]
+        out[8:16, pl.ds(base, CH)] = ref[:, CH : 2 * CH]
+        out[16:20, pl.ds(base, half)] = ref[0:4, 2 * CH : PW]
+        out[16:20, pl.ds(base + half, half)] = ref[4:8, 2 * CH : PW]
+
+    def place_back(c):
+        for d in (1, 3, 2):
+            back_landed(d, c).wait_recv()
+            place(orv.at[lax.rem(m + RANKS - d, RANKS), c], d, c)
+
+    def work(c):
         for d in (1, 3, 2):
             landed(d, c).wait_recv()
         e = unpack([rv[p, c] for p in range(RANKS)], CH)
-        where = first + c * CH + lax.broadcasted_iota(jnp.int32, (1, CH), 1)
-        pos = where.astype(F32) * (1.0 / LOC_C)
-        e = update(e, pos, p1[...], a1[...], w1[...])
-        e = update(e, pos, p2[...], a2[...], w2[...])
+        e = update(e, r1[c], a1[...], w1[...])
+        e = update(e, r2[c], a2[...], w2[...])
         for p, tiles in enumerate(pack(e)):
             for begin, tile in tiles:
                 rpk[p, c, :, begin : begin + tile.shape[1]] = tile
         for d in (1, 3, 2):
             back(d, c).start()
-        keep(c).start()
+        place(rpk.at[m, c], 0, c)
+
+    def work_first(c, _):
+        work(c)
         return 0
 
-    lax.fori_loop(0, NC, work, 0)
+    def work_later(c, _):
+        work(c)
+        place_back(c - LAG)
+        return 0
+
+    def place_rest(c, _):
+        place_back(c)
+        return 0
+
+    lax.fori_loop(0, LAG, work_first, 0)
+    lax.fori_loop(LAG, NC, work_later, 0)
+    lax.fori_loop(NC - LAG, NC, place_rest, 0)
 
     def finish(c, _):
         for d in (1, 3, 2):
             forward(d, c).wait_send()
             back(d, c).wait_send()
-            back_landed(d, c).wait_recv()
-        keep(c).wait()
         return 0
 
     lax.fori_loop(0, NC, finish, 0)
@@ -506,15 +547,13 @@
     dma = pltpu.SemaphoreType.DMA
     return pl.pallas_call(
         functools.partial(fused_kernel, mesh.shape["slab"]),
-        out_shape=(
-            jax.ShapeDtypeStruct((RANKS, NC, 8, PW), F32),
-            jax.ShapeDtypeStruct((1,), F32),
-        ),
+        out_shape=jax.ShapeDtypeStruct((MEMBERS // RANKS, SLAB), F32),
         in_specs=[sm, vm, vm, vm, vm, hbm],
-        out_specs=(hbm, sm),
+        out_specs=vm,
         scratch_shapes=[
             pltpu.VMEM((MEMBERS // RANKS, SLAB), F32),
             pltpu.VMEM((RANKS - 1, NC, 8, PW), F32),
+            pltpu.VMEM((RANKS, NC, 8, PW), F32),
             pltpu.VMEM((RANKS, NC, 8, PW), F32),
             pltpu.VMEM((RANKS, NC, 8, PW), F32),
             pltpu.VMEM((8, CW), F32),
@@ -523,15 +562,16 @@
             pltpu.VMEM((INNER, 3 * MEMBERS), BF16),
             pltpu.VMEM((2 * MEMBERS, INNER), BF16),
             pltpu.VMEM((INNER, 128), F32),
+            pltpu.VMEM((NC, INNER, CH), F32),
             pltpu.VMEM((INNER, 3 * MEMBERS), BF16),
             pltpu.VMEM((2 * MEMBERS, INNER), BF16),
             pltpu.VMEM((INNER, 128), F32),
+            pltpu.VMEM((NC, INNER, CH), F32),
             dma,
             dma((RANKS - 1, NC)),
             dma((RANKS - 1, NC)),
             dma((RANKS - 1, NC)),
             dma((RANKS - 1, NC)),
-            dma((NC,)),
             dma((RANKS - 1,)),
             dma((RANKS - 1,)),
             dma,
@@ -544,32 +584,26 @@
     )(batch_order, obs_value, obs_var, obs_slab, obs_offset, ensemble)
 
 
-def lay_kernel(got, out):
-    half = CH // 2
-    for c in range(got.shape[1]):
-        base = c * CH
-        out[0:8, base : base + CH] = got[0, c, :, 0:CH]
-        out[8:16, base : base + CH] = got[0, c, :, CH : 2 * CH]
-        out[16:20, base : base + half] = got[0, c, 0:4, 2 * CH : PW]
-        out[16:20, base + half : base + CH] = got[0, c, 4:8, 2 * CH : PW]
-
-
-def lay(got):
-    parts = 2
+def check_kernel(slab, off, bad):
+    bad[0] = count_over([slab[i : i + 1, :] * SLAB + off[i : i + 1, :] for i in range(NB)])
+
+
+def check(obs_slab, obs_offset):
+    vm = pl.BlockSpec(memory_space=pltpu.VMEM)
     return pl.pallas_call(
-        lay_kernel,
-        grid=(RANKS, parts),
-        out_shape=jax.ShapeDtypeStruct((MEMBERS // RANKS, SLAB), F32),
-        in_specs=[pl.BlockSpec((1, NC // parts, 8, PW), lambda p, h: (p, h, 0, 0))],
-        out_specs=pl.BlockSpec((MEMBERS // RANKS, SUB // parts), lambda p, h: (0, p * parts + h)),
-        name="lay",
-    )(got)
+        check_kernel,
+        out_shape=jax.ShapeDtypeStruct((1,), F32),
+        in_specs=[vm, vm],
+        out_specs=pl.BlockSpec(memory_space=pltpu.SMEM),
+        compiler_params=pltpu.CompilerParams(vmem_limit_bytes=32 << 20),
+        name="check",
+    )(obs_slab, obs_offset)
 
 
 def local(mesh, ensemble, obs_value, obs_var, obs_slab, obs_offset, batch_order):
     args = (ensemble, obs_value, obs_var, obs_slab, obs_offset, batch_order)
-    got, bad = fused(mesh, *args)
-    return lax.cond(bad[0] < 0.5, lambda: lay(got), lambda: general(*args))
+    bad = check(obs_slab, obs_offset)
+    return lax.cond(bad[0] < 0.5, lambda: fused(mesh, *args), lambda: general(*args))
 
 
 def solution(mesh):

time: 48.5 us -> 43.4 us (0.89)
  Pallas kernels: 46.2 us -> 40.9 us
    pallas_call x1, Pallas kernels: 42.2 us -> 39.1 us  [fused(): pl.pallas_call(functools.partial(fused_kernel, mesh.shape['slab']), out_s...]
    pallas_call x1, Pallas kernels: 4.01 us -> 1.83 us  [check(): pl.pallas_call(check_kernel, out_shape=jax.ShapeDtypeStruct((1,), F32), i...]
    unnamed x2 -> x1, local copies, waits for them, and re-layouts: 1.14 us -> 1.15 us
where the time goes in v3:
time: 43.4 us; the launch traced here: 43 us
  Pallas kernels  40.9 us (94%)
  local copies, waits for them, and re-layouts  1.15 us (3%)
  between operations  0.67 us (2%)
    pallas_call x1, Pallas kernels, fused(): pl.pallas_call(functools.partial(fused_kernel, mesh.shape['slab']), out_s...  39.1 us
    pallas_call x1, Pallas kernels, check(): pl.pallas_call(check_kernel, out_shape=jax.ShapeDtypeStruct((1,), F32), i...  1.83 us
    unnamed x1, local copies, waits for them, and re-layouts  1.15 us

profile of v3, /device:TPU:1, one launch (start us, length us, event | category | flops | bytes accessed | tf_op | source)
XLA Modules:
  0.0 43.0 jit_solution(3907144232776064541)
XLA Ops:
  0.0 1.8 %check.1 = f32[1]{0:T(128)} custom-call(s32[2,2048]{1,0:T(2,128)} %slab.1, s32[2,2048]{1,0:T(2,128)} %off.1), custom_call_target="tpu_custom_call" | custom-call | tf_op jit(solution)/shard_map/check/pallas_call | solution.py:593
  2.5 39.3 %conditional.1 = (f32[20,16384]{1,0:T(8,128)S(1)}) conditional(s32[]{:T(128)} %bitcast.16, (f32[20,16384]{1,0:T(8,128)}, s32[2]{0:T(128)}, s32[2,2048]{1,0:T(2,128)}, s32[2,2048]{1,0:T(2,128)}, f32[2,2048]{1,0:T(2,128)}, /*index=5*/f32[2,2048]{1,0:T(2,128)}) %tuple.56, (s32[2]{0:T(128)}, f32[2,2048]{1,0:T(2,128)}, f32[2,2048]{1,0:T(2,128)}, ...), branch_computations={%region_0.12_spmd, %region_11.13_spmd} | conditional | flops 4132327424 | bytes 175662432 | solution.py:606
  2.7 39.1 %fused.1 = f32[20,16384]{1,0:T(8,128)S(1)} custom-call(s32[2]{0:T(128)} %get-tuple-element.533.order, f32[2,2048]{1,0:T(2,128)} %get-tuple-element.534.val, f32[2,2048]{1,0:T(2,128)} %get-tuple-element.535.var, s32[2,2048]{1,0:T(2,128)} %get-tuple-element.536.slab, s32[2,2048]{1,0:T(2,128)} %get-tuple-element.537.off, f32[20,16384]{1,0:T(8,128)} %get-tuple-element.538.x_hbm), custom_call_target="tpu_custom_call" | custom-call | tf_op jit(solution)/shard_map/cond/branch_1_fun/fused/pallas_call | solution.py:548
  41.8 1.1 %copy.79 = f32[20,16384]{1,0:T(8,128)} copy(f32[20,16384]{1,0:T(8,128)S(1)} %get-tuple-element.539) | data formatting | bytes 2621440

commit v4 on v3

--- a/solution.py
+++ b/solution.py
@@ -151,12 +151,15 @@
 
 def count_over(loc_b):
     bad = jnp.zeros((8, 128), F32)
-    bins = lax.broadcasted_iota(jnp.int32, (128, OBS), 0)
+    bins = lax.broadcasted_iota(jnp.int32, (128, 128), 0)
     at = lax.broadcasted_iota(jnp.int32, (8, 128), 1)
     for loc in loc_b:
-        hot = jnp.where(bins == lax.shift_right_logical(loc, SUB_BITS), 1.0, 0.0).astype(BF16)
+        sub = lax.shift_right_logical(loc, SUB_BITS)
+        hits = jnp.zeros((128, 128), F32)
+        for b in range(OBS // 128):
+            hits = hits + jnp.where(bins == sub[:, b * 128 : (b + 1) * 128], 1.0, 0.0)
         cnt = lax.dot_general(
-            jnp.ones((8, OBS), BF16), hot, (((1,), (1,)), ((), ())), preferred_element_type=F32
+            jnp.ones((8, 128), BF16), hits.astype(BF16), (((1,), (1,)), ((), ())), preferred_element_type=F32
         )
         around = [pltpu.roll(cnt, sh, 1) for sh in (1, 127, 2, 126, 3)]
         near = cnt + around[0] + around[1]
@@ -248,8 +251,14 @@
     below = m < RANKS // 2
     send_to = lax.rem(s + jnp.where(below, 1, slabs - 1), slabs)
     gets_from = lax.rem(s + jnp.where(below, slabs - 1, 1), slabs)
-    load = pltpu.make_async_copy(x_hbm, x, xs)
-    load.start()
+
+    def load(p, part):
+        cols = pl.ds(p * SUB + part * EARLY * CH, (NC - EARLY if part else EARLY) * CH)
+        return pltpu.make_async_copy(x_hbm.at[:, cols], x.at[:, cols], xs.at[p, part])
+
+    for part in (0, 1):
+        for p in range(RANKS):
+            load(p, part).start()
 
     barrier = pltpu.get_barrier_semaphore()
     for d in range(1, RANKS):
@@ -278,7 +287,9 @@
         offs.append(lax.dot_general(both, hot, (((1,), (1,)), ((), ())), preferred_element_type=F32))
     offs = jnp.concatenate(offs, axis=1).astype(jnp.int32)
 
-    load.wait()
+    for p in range(RANKS):
+        load(p, 0).wait()
+        load(p, 1).wait()
     pl.semaphore_wait(barrier, RANKS)
 
     def fill(ref, base):
@@ -292,7 +303,7 @@
         return pltpu.make_async_remote_copy(
             src_ref=pk.at[d - 1, c],
             dst_ref=rv.at[m, c],
-            send_sem=fs.at[d - 1, c],
+            send_sem=fs.at[d - 1],
             recv_sem=fr.at[d - 1, c],
             device_id=(s, lax.rem(m + d, RANKS)),
             device_id_type=MESH,
@@ -302,20 +313,20 @@
         return pltpu.make_async_remote_copy(
             src_ref=pk.at[d - 1, c],
             dst_ref=rv.at[lax.rem(m + RANKS - d, RANKS), c],
-            send_sem=fs.at[d - 1, c],
+            send_sem=fs.at[d - 1],
             recv_sem=fr.at[d - 1, c],
             device_id=(s, lax.rem(m + d, RANKS)),
             device_id_type=MESH,
         )
 
     def fill_chunk(c):
-        for d in (1, 3, 2):
+        for d in (2, 1, 3):
             p = lax.rem(m + d, RANKS)
             fill(pk.at[d - 1, c], pl.multiple_of(p * SUB + c * CH, CH))
         fill(rv.at[m, c], pl.multiple_of(m * SUB + c * CH, CH))
 
     def send_chunk(c):
-        for d in (1, 3, 2):
+        for d in (2, 1, 3):
             forward(d, c).start()
 
     def first_chunks(c, _):
@@ -332,6 +343,7 @@
         return 0
 
     lax.fori_loop(0, EARLY, first_chunks, 0)
+
     lax.fori_loop(EARLY, NC, fill_later, 0)
 
     n = NB * OWN
@@ -360,7 +372,7 @@
 
     def pick_chunk(c, acc):
         acc = pick(rv.at[m, c], m * (SUB // 128) + c * per, acc)
-        for d in (1, 3, 2):
+        for d in (2, 1, 3):
             acc = pick(pk.at[d - 1, c], lax.rem(m + d, RANKS) * (SUB // 128) + c * per, acc)
         return acc
 
@@ -391,7 +403,7 @@
             device_id_type=MESH,
         )
 
-    for d in (1, 3, 2):
+    for d in (2, 1, 3):
         columns(d).start()
     crv[m] = cpk[...]
     lax.fori_loop(EARLY, MID, send_later, 0)
@@ -436,7 +448,7 @@
         lax.fori_loop(0, NC, step, 0)
 
     tapers(r1, p1)
-    for d in (1, 3, 2):
+    for d in (2, 1, 3):
         columns_landed(d).wait_recv()
     beside = pltpu.make_async_remote_copy(
         src_ref=crv, dst_ref=nrv, send_sem=ns, recv_sem=nr, device_id=(send_to, m), device_id_type=MESH
@@ -469,7 +481,7 @@
         return pltpu.make_async_remote_copy(
             src_ref=rpk.at[lax.rem(m + d, RANKS), c],
             dst_ref=orv.at[m, c],
-            send_sem=bs.at[d - 1, c],
+            send_sem=bs.at[d - 1],
             recv_sem=br.at[d - 1, c],
             device_id=(s, lax.rem(m + d, RANKS)),
             device_id_type=MESH,
@@ -479,7 +491,7 @@
         return pltpu.make_async_remote_copy(
             src_ref=rpk.at[lax.rem(m + d, RANKS), c],
             dst_ref=orv.at[lax.rem(m + RANKS - d, RANKS), c],
-            send_sem=bs.at[d - 1, c],
+            send_sem=bs.at[d - 1],
             recv_sem=br.at[d - 1, c],
             device_id=(s, lax.rem(m + d, RANKS)),
             device_id_type=MESH,
@@ -494,12 +506,12 @@
         out[16:20, pl.ds(base + half, half)] = ref[4:8, 2 * CH : PW]
 
     def place_back(c):
-        for d in (1, 3, 2):
+        for d in (2, 1, 3):
             back_landed(d, c).wait_recv()
             place(orv.at[lax.rem(m + RANKS - d, RANKS), c], d, c)
 
     def work(c):
-        for d in (1, 3, 2):
+        for d in (2, 1, 3):
             landed(d, c).wait_recv()
         e = unpack([rv[p, c] for p in range(RANKS)], CH)
         e = update(e, r1[c], a1[...], w1[...])
@@ -507,7 +519,7 @@
         for p, tiles in enumerate(pack(e)):
             for begin, tile in tiles:
                 rpk[p, c, :, begin : begin + tile.shape[1]] = tile
-        for d in (1, 3, 2):
+        for d in (2, 1, 3):
             back(d, c).start()
         place(rpk.at[m, c], 0, c)
 
@@ -528,14 +540,14 @@
     lax.fori_loop(LAG, NC, work_later, 0)
     lax.fori_loop(NC - LAG, NC, place_rest, 0)
 
-    def finish(c, _):
-        for d in (1, 3, 2):
-            forward(d, c).wait_send()
-            back(d, c).wait_send()
-        return 0
-
-    lax.fori_loop(0, NC, finish, 0)
-    for d in (1, 3, 2):
+    for d in (2, 1, 3):
+        there = (s, lax.rem(m + d, RANKS))
+        mine = rpk.at[lax.rem(m + d, RANKS)]
+        for ref, sem in ((pk.at[d - 1], fs.at[d - 1]), (mine, bs.at[d - 1])):
+            pltpu.make_async_remote_copy(
+                src_ref=ref, dst_ref=ref, send_sem=sem, recv_sem=nr, device_id=there, device_id_type=MESH
+            ).wait_send()
+    for d in (2, 1, 3):
         columns(d).wait_send()
     beside.wait_send()
 
@@ -567,10 +579,10 @@
             pltpu.VMEM((2 * MEMBERS, INNER), BF16),
             pltpu.VMEM((INNER, 128), F32),
             pltpu.VMEM((NC, INNER, CH), F32),
-            dma,
+            dma((RANKS, 2)),
+            dma((RANKS - 1,)),
             dma((RANKS - 1, NC)),
-            dma((RANKS - 1, NC)),
-            dma((RANKS - 1, NC)),
+            dma((RANKS - 1,)),
             dma((RANKS - 1, NC)),
             dma((RANKS - 1,)),
             dma((RANKS - 1,)),

time: 43.4 us -> 42.7 us (0.984)
  Pallas kernels: 40.9 us -> 40 us
    pallas_call x1, Pallas kernels: 39.1 us -> 38.3 us  [fused(): pl.pallas_call(functools.partial(fused_kernel, mesh.shape['slab']), out_s...]
where the time goes in v4:
time: 42.7 us; the launch traced here: 42.1 us
  Pallas kernels  40 us (94%)
  local copies, waits for them, and re-layouts  1.15 us (3%)
  between operations  0.67 us (2%)
    pallas_call x1, Pallas kernels, fused(): pl.pallas_call(functools.partial(fused_kernel, mesh.shape['slab']), out_s...  38.3 us
    pallas_call x1, Pallas kernels, check(): pl.pallas_call(check_kernel, out_shape=jax.ShapeDtypeStruct((1,), F32), i...  1.78 us
    unnamed x1, local copies, waits for them, and re-layouts  1.15 us

profile of v4, /device:TPU:1, one launch (start us, length us, event | category | flops | bytes accessed | tf_op | source)
XLA Modules:
  0.0 42.1 jit_solution(4648641648532067577)
XLA Ops:
  0.0 1.8 %check.1 = f32[1]{0:T(128)} custom-call(s32[2,2048]{1,0:T(2,128)} %slab.1, s32[2,2048]{1,0:T(2,128)} %off.1), custom_call_target="tpu_custom_call" | custom-call | tf_op jit(solution)/shard_map/check/pallas_call | solution.py:605
  2.4 38.5 %conditional.1 = (f32[20,16384]{1,0:T(8,128)S(1)}) conditional(s32[]{:T(128)} %bitcast.16, (f32[20,16384]{1,0:T(8,128)}, s32[2]{0:T(128)}, s32[2,2048]{1,0:T(2,128)}, s32[2,2048]{1,0:T(2,128)}, f32[2,2048]{1,0:T(2,128)}, /*index=5*/f32[2,2048]{1,0:T(2,128)}) %tuple.56, (s32[2]{0:T(128)}, f32[2,2048]{1,0:T(2,128)}, f32[2,2048]{1,0:T(2,128)}, ...), branch_computations={%region_0.12_spmd, %region_11.13_spmd} | conditional | flops 4132327424 | bytes 175662432 | solution.py:618
  2.7 38.3 %fused.1 = f32[20,16384]{1,0:T(8,128)S(1)} custom-call(s32[2]{0:T(128)} %get-tuple-element.533.order, f32[2,2048]{1,0:T(2,128)} %get-tuple-element.534.val, f32[2,2048]{1,0:T(2,128)} %get-tuple-element.535.var, s32[2,2048]{1,0:T(2,128)} %get-tuple-element.536.slab, s32[2,2048]{1,0:T(2,128)} %get-tuple-element.537.off, f32[20,16384]{1,0:T(8,128)} %get-tuple-element.538.x_hbm), custom_call_target="tpu_custom_call" | custom-call | tf_op jit(solution)/shard_map/cond/branch_1_fun/fused/pallas_call | solution.py:560
  40.9 1.1 %copy.79 = f32[20,16384]{1,0:T(8,128)} copy(f32[20,16384]{1,0:T(8,128)S(1)} %get-tuple-element.539) | data formatting | bytes 2621440

commit v5 on v4

--- a/solution.py
+++ b/solution.py
@@ -27,6 +27,7 @@
 EARLY = 2
 MID = 4
 LAG = 4
+AHEAD = 4
 FAR = -1.0e5
 MESH = pl.DeviceIdType.MESH
 F32 = jnp.float32
@@ -319,23 +320,27 @@
             device_id_type=MESH,
         )
 
-    def fill_chunk(c):
+    def fill_one(d, c):
+        p = lax.rem(m + d, RANKS)
+        fill(pk.at[d - 1, c] if d else rv.at[m, c], pl.multiple_of(p * SUB + c * CH, CH))
+
+    def first_chunks(c, _):
         for d in (2, 1, 3):
-            p = lax.rem(m + d, RANKS)
-            fill(pk.at[d - 1, c], pl.multiple_of(p * SUB + c * CH, CH))
-        fill(rv.at[m, c], pl.multiple_of(m * SUB + c * CH, CH))
+            fill_one(d, c)
+            forward(d, c).start()
+        return 0
+
+    def fill_own(c, _):
+        fill_one(0, c)
+        return 0
 
     def send_chunk(c):
         for d in (2, 1, 3):
             forward(d, c).start()
 
-    def first_chunks(c, _):
-        fill_chunk(c)
-        send_chunk(c)
-        return 0
-
     def fill_later(c, _):
-        fill_chunk(c)
+        for d in (2, 1, 3):
+            fill_one(d, c)
         return 0
 
     def send_later(c, _):
@@ -345,6 +350,7 @@
     lax.fori_loop(0, EARLY, first_chunks, 0)
 
     lax.fori_loop(EARLY, NC, fill_later, 0)
+    lax.fori_loop(0, NC, fill_own, 0)
 
     n = NB * OWN
     at = lax.broadcasted_iota(jnp.int32, (128, n), 0)
@@ -440,14 +446,17 @@
     p1[...] = pv[:INNER]
     p2[...] = column(prm[1][0])
 
-    def tapers(dst, src):
+    def taper_of(c, src):
+        return reach(here + c.astype(F32) * (CH / LOC_C), src[...])
+
+    def tapers(dst, src, begin, end):
         def step(c, _):
-            dst[c] = reach(here + c.astype(F32) * (CH / LOC_C), src[...])
+            dst[c] = taper_of(c, src)
             return 0
 
-        lax.fori_loop(0, NC, step, 0)
-
-    tapers(r1, p1)
+        lax.fori_loop(begin, end, step, 0)
+
+    tapers(r1, p1, 0, AHEAD)
     for d in (2, 1, 3):
         columns_landed(d).wait_recv()
     beside = pltpu.make_async_remote_copy(
@@ -455,7 +464,8 @@
     )
     beside.start()
     lax.fori_loop(MID, NC, send_later, 0)
-    tapers(r2, p2)
+    tapers(r1, p1, AHEAD, NC)
+    tapers(r2, p2, 0, LAG)
     own_cols = unpack([crv[p] for p in range(RANKS)], NB * OWN)
     beside.wait_recv()
     nb_cols = unpack([nrv[p] for p in range(RANKS)], NB * OWN)
@@ -510,12 +520,12 @@
             back_landed(d, c).wait_recv()
             place(orv.at[lax.rem(m + RANKS - d, RANKS), c], d, c)
 
-    def work(c):
+    def work(c, late):
         for d in (2, 1, 3):
             landed(d, c).wait_recv()
         e = unpack([rv[p, c] for p in range(RANKS)], CH)
         e = update(e, r1[c], a1[...], w1[...])
-        e = update(e, r2[c], a2[...], w2[...])
+        e = update(e, taper_of(c, p2) if late else r2[c], a2[...], w2[...])
         for p, tiles in enumerate(pack(e)):
             for begin, tile in tiles:
                 rpk[p, c, :, begin : begin + tile.shape[1]] = tile
@@ -524,11 +534,11 @@
         place(rpk.at[m, c], 0, c)
 
     def work_first(c, _):
-        work(c)
+        work(c, False)
         return 0
 
     def work_later(c, _):
-        work(c)
+        work(c, True)
         place_back(c - LAG)
         return 0
 

time: 42.7 us -> 42.7 us (level)
  no operation moved by 1% of the time
where the time goes in v5:
time: 42.7 us; the launch traced here: 42.1 us
  Pallas kernels  40.1 us (94%)
  local copies, waits for them, and re-layouts  1.15 us (3%)
  between operations  0.67 us (2%)
    pallas_call x1, Pallas kernels, fused(): pl.pallas_call(functools.partial(fused_kernel, mesh.shape['slab']), out_s...  38.3 us
    pallas_call x1, Pallas kernels, check(): pl.pallas_call(check_kernel, out_shape=jax.ShapeDtypeStruct((1,), F32), i...  1.78 us
    unnamed x1, local copies, waits for them, and re-layouts  1.15 us

profile of v5, /device:TPU:1, one launch (start us, length us, event | category | flops | bytes accessed | tf_op | source)
XLA Modules:
  0.0 42.1 jit_solution(913891100496746888)
XLA Ops:
  0.0 1.8 %check.1 = f32[1]{0:T(128)} custom-call(s32[2,2048]{1,0:T(2,128)} %slab.1, s32[2,2048]{1,0:T(2,128)} %off.1), custom_call_target="tpu_custom_call" | custom-call | tf_op jit(solution)/shard_map/check/pallas_call | solution.py:615
  2.4 38.5 %conditional.1 = (f32[20,16384]{1,0:T(8,128)S(1)}) conditional(s32[]{:T(128)} %bitcast.16, (f32[20,16384]{1,0:T(8,128)}, s32[2]{0:T(128)}, s32[2,2048]{1,0:T(2,128)}, s32[2,2048]{1,0:T(2,128)}, f32[2,2048]{1,0:T(2,128)}, /*index=5*/f32[2,2048]{1,0:T(2,128)}) %tuple.56, (s32[2]{0:T(128)}, f32[2,2048]{1,0:T(2,128)}, f32[2,2048]{1,0:T(2,128)}, ...), branch_computations={%region_0.12_spmd, %region_11.13_spmd} | conditional | flops 4132327424 | bytes 175662432 | solution.py:628
  2.7 38.3 %fused.1 = f32[20,16384]{1,0:T(8,128)S(1)} custom-call(s32[2]{0:T(128)} %get-tuple-element.533.order, f32[2,2048]{1,0:T(2,128)} %get-tuple-element.534.val, f32[2,2048]{1,0:T(2,128)} %get-tuple-element.535.var, s32[2,2048]{1,0:T(2,128)} %get-tuple-element.536.slab, s32[2,2048]{1,0:T(2,128)} %get-tuple-element.537.off, f32[20,16384]{1,0:T(8,128)} %get-tuple-element.538.x_hbm), custom_call_target="tpu_custom_call" | custom-call | tf_op jit(solution)/shard_map/cond/branch_1_fun/fused/pallas_call | solution.py:570
  41.0 1.1 %copy.79 = f32[20,16384]{1,0:T(8,128)} copy(f32[20,16384]{1,0:T(8,128)S(1)} %get-tuple-element.539) | data formatting | bytes 2621440

commit v6 on v4

--- a/solution.py
+++ b/solution.py
@@ -20,13 +20,13 @@
 OWN = 256
 INNER = 256
 OUTER = 128
-CH = 512
+CH = 1024
 NC = SUB // CH
 PW = CH * 5 // 2
 CW = 2 * OWN * 5 // 2
-EARLY = 2
-MID = 4
-LAG = 4
+EARLY = 1
+MID = 2
+LAG = 2
 FAR = -1.0e5
 MESH = pl.DeviceIdType.MESH
 F32 = jnp.float32

time: 42.7 us -> 42.4 us (level)
  no operation moved by 1% of the time
where the time goes in v6:
time: 42.4 us; the launch traced here: 42 us
  Pallas kernels  40 us (94%)
  local copies, waits for them, and re-layouts  1.15 us (3%)
  between operations  0.67 us (2%)
    pallas_call x1, Pallas kernels, fused(): pl.pallas_call(functools.partial(fused_kernel, mesh.shape['slab']), out_s...  38.2 us
    pallas_call x1, Pallas kernels, check(): pl.pallas_call(check_kernel, out_shape=jax.ShapeDtypeStruct((1,), F32), i...  1.78 us
    unnamed x1, local copies, waits for them, and re-layouts  1.15 us

profile of v6, /device:TPU:1, one launch (start us, length us, event | category | flops | bytes accessed | tf_op | source)
XLA Modules:
  0.0 42.0 jit_solution(6478521362539578383)
XLA Ops:
  0.0 1.8 %check.1 = f32[1]{0:T(128)} custom-call(s32[2,2048]{1,0:T(2,128)} %slab.1, s32[2,2048]{1,0:T(2,128)} %off.1), custom_call_target="tpu_custom_call" | custom-call | tf_op jit(solution)/shard_map/check/pallas_call | solution.py:605
  2.4 38.4 %conditional.1 = (f32[20,16384]{1,0:T(8,128)S(1)}) conditional(s32[]{:T(128)} %bitcast.16, (f32[20,16384]{1,0:T(8,128)}, s32[2]{0:T(128)}, s32[2,2048]{1,0:T(2,128)}, s32[2,2048]{1,0:T(2,128)}, f32[2,2048]{1,0:T(2,128)}, /*index=5*/f32[2,2048]{1,0:T(2,128)}) %tuple.56, (s32[2]{0:T(128)}, f32[2,2048]{1,0:T(2,128)}, f32[2,2048]{1,0:T(2,128)}, ...), branch_computations={%region_0.12_spmd, %region_11.13_spmd} | conditional | flops 4132327424 | bytes 175662432 | solution.py:618
  2.7 38.2 %fused.1 = f32[20,16384]{1,0:T(8,128)S(1)} custom-call(s32[2]{0:T(128)} %get-tuple-element.533.order, f32[2,2048]{1,0:T(2,128)} %get-tuple-element.534.val, f32[2,2048]{1,0:T(2,128)} %get-tuple-element.535.var, s32[2,2048]{1,0:T(2,128)} %get-tuple-element.536.slab, s32[2,2048]{1,0:T(2,128)} %get-tuple-element.537.off, f32[20,16384]{1,0:T(8,128)} %get-tuple-element.538.x_hbm), custom_call_target="tpu_custom_call" | custom-call | tf_op jit(solution)/shard_map/cond/branch_1_fun/fused/pallas_call | solution.py:560
  40.9 1.1 %copy.79 = f32[20,16384]{1,0:T(8,128)} copy(f32[20,16384]{1,0:T(8,128)S(1)} %get-tuple-element.539) | data formatting | bytes 2621440
